TPU v7x, 256 devices: a whole 4x4x8 slice. The times are simulated.
256 devices in a mesh: row: 64 (over y, z, core), col: 4 (over x).
Axes of the slice: x: 4, y: 4, z: 8, core: 2. Of those that a mesh axis runs over, the one named last changes fastest.
Arguments:
- a_tiles: bfloat16 [1024, 27, 128, 128], P('row'), may hold values from -0.109375 to 0.109375
- a_cols: int32 [1024, 27], P('row'), may hold values from 0 to 19, as said below
- p_tiles: bfloat16 [1024, 4, 128, 128], P('row', 'col'), may hold values from -2 to 2
- p_cols: int32 [1024, 4], P('row', 'col'), may hold values from 0 to 127, as said below
- send_rows: int32 [128, 2], P('row'), may hold values from 0 to 15, as said below
Outputs:
- coarse_matrix: float32 [128, 128, 128, 128], P('row', 'col')
Inputs may be any that keep to these rules, and one draw needn't show every extreme that they name: `a_cols`: an entry below 16 names a fine block row of the device's own slab; an entry 16 + t with t < 2 names the t-th row that the previous slab sends to this slab, and 18 + t the t-th row that the next slab sends to it. Every slab reads all 4 rows that it receives. Slabs are periodic. `p_cols`: the coarse block column of slot k in fine block row i is congruent to k modulo 4 and lies among the 6 consecutive ids that start at ((i div 16) - 1) * 2, modulo 128. `send_rows`: each row lists 2 distinct slab-local rows.
All inputs are finite; a program needn't handle non-finite values.
Results may differ from a plain program's by a relative error of at most 0.0029.
Values may be sent and summed in bfloat16 or wider, within the bound.
No kernel may reach another device: no remote copies, remote signals or barrier semaphores. Data moves between devices by JAX's collectives and lax.ppermute only.
A program may use at most 192 MiB of HBM per device.

v0:
```python
import functools

import jax
import jax.numpy as jnp
from jax import lax
from jax.experimental import pallas as pl
from jax.experimental.pallas import tpu as pltpu
from jax.sharding import PartitionSpec as P

T = 128
BR = 16
KA = 27
G = 3
UNROLL = 2
NCC = 32
F32 = jnp.float32
BF16 = jnp.bfloat16
MB = 1 << 20
SMEM = pl.BlockSpec(memory_space=pltpu.SMEM)
VMEM = pl.BlockSpec(memory_space=pltpu.VMEM)
HBM = pl.BlockSpec(memory_space=pl.ANY)
FIXED = pl.BlockSpec(memory_space=pltpu.HBM)


def place():
    s = lax.axis_index("row")
    c = lax.axis_index("col")
    d = lax.rem(c - 2 * s + 512, 4)
    is_n = d >= 2
    number = lax.rem(d, 2)
    return s, is_n, number, 2 * s - 4 + d


def roles(s):
    return (2, 3, 1, 0) if s % 2 == 0 else (0, 1, 3, 2)


def send(block, routes, rows, cols):
    pairs = []
    for s in range(rows):
        at = roles(s)
        pairs += [(s * cols + at[i], s * cols + at[j]) for i, j in routes]
    return lax.ppermute(block, ("row", "col"), pairs)


def swap_rows(block, odd, rows, cols):
    pairs = [(s, (s + 1) % rows if s % 2 == odd else (s - 1) % rows) for s in range(rows)]
    return lax.ppermute(block, "row", pairs)


N1, N2, L1, L2 = range(4)


def note_kernel(ids_ref, p_ref, all_ref, sem):
    copy = pltpu.make_async_copy(p_ref, all_ref.at[pl.ds(0, BR)], sem)
    copy.start()
    for i in range(BR):
        all_ref[BR, 8 * i:8 * i + 8, :] = jnp.full((8, T), ids_ref[i].astype(F32), F32).astype(BF16)
    copy.wait()


def pick_kernel(send_ref, p_ref, near_ref, far_ref, sems):
    odd = lax.rem(lax.axis_index("row"), 2)
    copies = []
    for d, out in ((odd, near_ref), (1 - odd, far_ref)):
        for t in range(2):
            row = send_ref[d, t]
            copies.append(pltpu.make_async_copy(p_ref.at[row], out.at[t], sems.at[len(copies)]))
            copies.append(pltpu.make_async_copy(p_ref.at[BR, pl.ds(pl.multiple_of(row * 8, 8), 8)],
                                                out.at[2, pl.ds(t * 8, 8)], sems.at[len(copies)]))
    for copy in copies:
        copy.start()
    for copy in copies:
        copy.wait()


def product_kernel(cols_ref, ids_ref, a_ref, own_ref, near_ref, far_ref, sums_ref, tiles, right, own, ghosts, sems):
    early = [pltpu.make_async_copy(own_ref.at[pl.ds(0, BR)], own, sems.at[BR]),
             pltpu.make_async_copy(near_ref, ghosts.at[0], sems.at[BR + 1]),
             pltpu.make_async_copy(far_ref, ghosts.at[1], sems.at[BR + 2])]
    for copy in early:
        copy.start()
    for i in range(BR):
        pltpu.make_async_copy(a_ref.at[i], tiles.at[i], sems.at[i]).start()
    s, is_n, number, first = place()
    right[...] = jnp.zeros_like(right)
    for copy in early:
        copy.wait()
    for j in range(BR):
        group = lax.rem(ids_ref[j] - first + 512, T) // 4
        right[j * G + group] = own[j]
    odd = lax.rem(s, 2)
    for side in range(2):
        base = BR + 2 * (1 - odd if side == 0 else odd)
        for t in range(2):
            ids = ghosts[side, 2, 8 * t:8 * t + 8, :].astype(F32)[:1]
            tile = ghosts[side, t].astype(F32)
            for g in range(G):
                wanted = lax.rem(first + 4 * g + T, T).astype(F32)
                right[(base + t) * G + g] = jnp.where(ids == wanted, tile, 0.0).astype(BF16)

    def one(i):
        pltpu.make_async_copy(a_ref.at[i], tiles.at[i], sems.at[i]).wait()
        rows = [cols_ref[i, m] * G for m in range(KA)]
        left = jnp.concatenate([tiles[i, m] for m in range(KA)], axis=1)
        both = jnp.concatenate(
            [jnp.concatenate([right[j + g] for g in range(G)], axis=1) for j in rows], axis=0)
        acc = jnp.dot(left, both, preferred_element_type=F32)
        turned = jnp.concatenate([acc[:, g * T:(g + 1) * T].T for g in range(G)], axis=0)
        sums_ref[i] = turned.astype(BF16)

    def step(n, _):
        for k in range(UNROLL):
            one(UNROLL * n + k)
        return 0

    lax.fori_loop(0, BR // UNROLL, step, 0)


def wide(ref):
    return jnp.concatenate([ref[i] for i in range(BR)], axis=1)


def partial_kernel(sums_ref, own, swapped, across, crossed, near_ref, far_ref, tiles, masked, sems):
    s, is_n, number, first = place()

    @pl.when(is_n)
    def _():
        for n, src in enumerate((own, swapped)):
            pltpu.make_async_copy(src, tiles.at[n], sems.at[n]).start()

    @pl.when(jnp.logical_not(is_n))
    def _():
        for n, src in enumerate((across, crossed)):
            pltpu.make_async_copy(src, tiles.at[n], sems.at[n]).start()

    sums = wide(sums_ref)
    odd = lax.rem(s, 2) == 1
    first_row = jnp.where(is_n, number, 1 - number)
    for n in range(2):
        pltpu.make_async_copy(own, tiles.at[n], sems.at[n]).wait()
        row = first_row if n == 0 else 1 - first_row
        wanted = lax.rem(2 * s - 2 + row + T, T).astype(F32)
        for i in range(BR):
            lower = tiles[n, BR, 8 * i:8 * i + 8, :].astype(F32)[:1] == wanted
            tile = tiles[n, i].astype(F32)
            masked[n, i * T:(i + 1) * T, :T] = jnp.where(lower, tile, 0.0).astype(BF16)
            masked[n, i * T:(i + 1) * T, T:] = jnp.where(lower, 0.0, tile).astype(BF16)
        terms = jnp.dot(sums, masked[n], preferred_element_type=F32)
        near_ref[row] = jnp.where(odd, terms[:, :T], terms[:, T:])
        far_ref[row] = jnp.where(odd, terms[:, T:], terms[:, :T])


def local_kernel(sums_ref, own, swapped, across, crossed, after, out_ref, total_ref, tiles, zeros, sems):
    del after
    s, is_n, number, first = place()

    @pl.when(is_n)
    def _():
        for n, src in enumerate((across, crossed)):
            pltpu.make_async_copy(src, tiles.at[n], sems.at[n]).start()

    @pl.when(jnp.logical_not(is_n))
    def _():
        for n, src in enumerate((own, swapped)):
            pltpu.make_async_copy(src, tiles.at[n], sems.at[n]).start()

    zeros[...] = jnp.zeros_like(zeros)
    copies = [pltpu.make_async_copy(zeros, out_ref.at[r, pl.ds(q, 8)], sems.at[2 + r * 4 + q // 8])
              for r in range(2) for q in range(0, NCC, 8)]
    for copy in copies:
        copy.start()
    total_ref[...] = jnp.zeros_like(total_ref)
    sums = wide(sums_ref)
    at = pl.ds(pl.multiple_of(is_n.astype(jnp.int32) * T, T), G * T)
    first_row = jnp.where(is_n, 1 - number, number)
    for n in range(2):
        pltpu.make_async_copy(own, tiles.at[n], sems.at[n]).wait()
        right = tiles[n, :BR].reshape(BR * T, T)
        row = first_row if n == 0 else 1 - first_row
        total_ref[row, at, :] = jnp.dot(sums, right, preferred_element_type=F32)
    for copy in copies:
        copy.wait()


def final_kernel(total_ref, near_ref, far_ref, zeroed, out_ref, blocks, sems):
    del zeroed
    s, is_n, number, first = place()
    base = jnp.where(is_n, first - 4, first)
    odd = lax.rem(s, 2) == 1
    copies = []
    for r in range(2):
        for q in range(4):
            block = total_ref[r, q * T:(q + 1) * T, :]
            if q < G:
                at = slice(q * T, (q + 1) * T)
                block += jnp.where(odd, near_ref[r, at, :], far_ref[r, at, :])
            if q > 0:
                at = slice((q - 1) * T, q * T)
                block += jnp.where(odd, far_ref[r, at, :], near_ref[r, at, :])
            blocks[r, q] = block.T
            column = lax.rem(base + 4 * q + T, T) // 4
            copy = pltpu.make_async_copy(blocks.at[r, q], out_ref.at[r, column], sems.at[r * 4 + q])
            copy.start()
            copies.append(copy)
    for copy in copies:
        copy.wait()


def params(mib):
    return pltpu.CompilerParams(vmem_limit_bytes=mib * MB)


def cost(flops, count):
    return pl.CostEstimate(flops=flops, bytes_accessed=count, transcendentals=0)


def shards(rows, cols, a_tiles, a_cols, p_tiles, p_cols, send_rows):
    go = functools.partial(send, rows=rows, cols=cols)
    own = p_tiles.reshape(BR, T, T)
    ids = p_cols.reshape(BR)
    noted = pl.pallas_call(
        note_kernel, out_shape=jax.ShapeDtypeStruct((BR + 1, T, T), BF16), in_specs=[SMEM, FIXED], out_specs=VMEM,
        scratch_shapes=[pltpu.SemaphoreType.DMA], compiler_params=params(8), name="note",
    )(ids, own)
    swapped = go(noted, ((N1, N2), (N2, N1), (L1, L2), (L2, L1)))
    across = go(noted, ((N1, L1), (N2, L2), (L1, N1), (L2, N2)))
    crossed = go(noted, ((N1, L2), (N2, L1), (L1, N2), (L2, N1)))
    swapped_late, across_late, crossed_late = swapped, across, crossed
    ghost = jax.ShapeDtypeStruct((3, T, T), BF16)
    near, far = pl.pallas_call(
        pick_kernel, out_shape=(ghost, ghost), in_specs=[SMEM, HBM], out_specs=(VMEM, VMEM),
        scratch_shapes=[pltpu.SemaphoreType.DMA((8,))], compiler_params=params(8), name="pick",
    )(send_rows, noted)
    near, far = swap_rows(near, 0, rows, cols), swap_rows(far, 1, rows, cols)
    sums = pl.pallas_call(
        product_kernel, out_shape=jax.ShapeDtypeStruct((BR, G * T, T), BF16),
        in_specs=[SMEM, SMEM, FIXED, HBM, HBM, HBM], out_specs=VMEM,
        scratch_shapes=[pltpu.VMEM((BR, KA, T, T), BF16), pltpu.VMEM(((BR + 4) * G, T, T), BF16),
                        pltpu.VMEM((BR, T, T), BF16), pltpu.VMEM((2, 3, T, T), BF16),
                        pltpu.SemaphoreType.DMA((BR + 3,))],
        compiler_params=params(50), cost_estimate=cost(7_000_000_000, 15_000_000), name="products",
    )(a_cols, ids, a_tiles, noted, near, far)
    travels = jax.ShapeDtypeStruct((2, G * T, T), F32)
    near, far = pl.pallas_call(
        partial_kernel, out_shape=(travels, travels), in_specs=[VMEM] + [HBM] * 4, out_specs=(VMEM, VMEM),
        scratch_shapes=[pltpu.VMEM((2, BR + 1, T, T), BF16), pltpu.VMEM((2, BR * T, 2 * T), BF16),
                        pltpu.SemaphoreType.DMA((2,))],
        compiler_params=params(24), name="partials",
    )(sums, noted, swapped, across, crossed)
    near_sum, far_sum = swap_rows(near, 0, rows, cols), swap_rows(far, 1, rows, cols)
    out = jax.ShapeDtypeStruct((2, NCC, T, T), F32)
    zeroed, total = pl.pallas_call(
        local_kernel, out_shape=(out, jax.ShapeDtypeStruct((2, 4 * T, T), F32)),
        in_specs=[VMEM] + [HBM] * 5, out_specs=(HBM, VMEM),
        scratch_shapes=[pltpu.VMEM((2, BR + 1, T, T), BF16), pltpu.VMEM((8, T, T), F32),
                        pltpu.SemaphoreType.DMA((10,))],
        compiler_params=params(24), name="local",
    )(sums, noted, swapped_late, across_late, crossed_late, near)
    return pl.pallas_call(
        final_kernel, out_shape=out, in_specs=[VMEM] * 3 + [HBM], out_specs=HBM,
        scratch_shapes=[pltpu.VMEM((2, 4, T, T), F32), pltpu.SemaphoreType.DMA((8,))],
        input_output_aliases={3: 0}, compiler_params=params(24), name="final",
    )(total, near_sum, far_sum, zeroed)


def solution(mesh):
    in_specs = (P("row", None, None, None), P("row", None), P("row", "col", None, None), P("row", "col"), P("row", None))
    body = functools.partial(shards, mesh.shape["row"], mesh.shape["col"])
    return jax.shard_map(body, mesh=mesh, in_specs=in_specs, out_specs=P("row", "col", None, None), check_vma=False)
```

profile of v0, /device:TPU:6, one launch (start us, length us, event | category | flops | bytes accessed | tf_op | source)
XLA Modules:
  0.0 49.9 jit_solution(12058052659766146035)
XLA Ops:
  0.0 0.0 copy-start
  0.0 1.0 %copy-done = bf16[16,1,128,128]{3,2,1,0:T(8,128)(2,1)S(1)} copy-done((bf16[16,1,128,128]{3,2,1,0:T(8,128)(2,1)S(1)}, bf16[16,1,128,128]{3,2,1,0:T(8,128)(2,1)}, u32[]{:S(2)}) %copy-start) | copy-done | bytes 524312
  1.0 0.0 copy-start.2
  1.0 0.7 %copy-done.2 = s32[16,1]{0,1:T(1,128)S(1)} copy-done((s32[16,1]{0,1:T(1,128)S(1)}, s32[16,1]{0,1:T(1,128)}, u32[]{:S(2)}) %copy-start.2) | copy-done | bytes 88
  1.7 0.6 %note.1.p_ref.own_ref.own = bf16[17,128,128]{2,1,0:T(8,128)(2,1)S(1)} custom-call(s32[16]{0:T(128)S(1)} %bitcast.3, bf16[16,128,128]{2,1,0:T(8,128)(2,1)S(1)} %bitcast.2), custom_call_target="tpu_custom_call" | custom-call | tf_op jit(solution)/shard_map/note/pallas_call | solution.py:222
  2.3 0.0 copy-start.1
  2.3 0.7 %copy-done.1 = s32[2,2]{1,0:T(2,128)S(1)} copy-done((s32[2,2]{1,0:T(2,128)S(1)}, s32[2,2]{1,0:T(2,128)}, u32[]{:S(2)}) %copy-start.1) | copy-done | bytes 40
  3.0 0.8 %pick.1 = (bf16[3,128,128]{2,1,0:T(8,128)(2,1)S(1)}, bf16[3,128,128]{2,1,0:T(8,128)(2,1)S(1)}) custom-call(s32[2,2]{1,0:T(2,128)S(1)} %copy-done.1, bf16[17,128,128]{2,1,0:T(8,128)(2,1)S(1)} %note.1.p_ref.own_ref.own), custom_call_target="tpu_custom_call" | custom-call | tf_op jit(solution)/shard_map/pick/pallas_call | solution.py:231
  3.8 0.1 collective-permute-start
  3.9 8.4 %collective-permute-start.1 = (bf16[3,128,128]{2,1,0:T(8,128)(2,1)S(1)}, bf16[3,128,128]{2,1,0:T(8,128)(2,1)S(1)}, u32[]{:S(2)}, u32[]{:S(2)}) collective-permute-start(bf16[3,128,128]{2,1,0:T(8,128)(2,1)S(1)} %get-tuple-element.12), channel_id=1, source_target_pairs={{0,252},{4,8},{8,4},{12,16},{16,12},{20,24},{24,20},{28,32},{32,28... | collective-permute-start | bytes 294920 | tf_op jit(solution)/shard_map/ppermute | solution.py:48
  12.3 0.8 %collective-permute-start.2 = (bf16[17,128,128]{2,1,0:T(8,128)(2,1)S(1)}, bf16[17,128,128]{2,1,0:T(8,128)(2,1)S(1)}, u32[]{:S(2)}, u32[]{:S(2)}) collective-permute-start(bf16[17,128,128]{2,1,0:T(8,128)(2,1)S(1)} %note.1.p_ref.own_ref.own), channel_id=1, source_target_pairs={{2,3},{3,2},{1,0},{0,1},{4,5},{5,4},{7,6},{6,7},{10,11},{11,10},{9... | collective-permute-start | bytes 1671176 | tf_op jit(solution)/shard_map/ppermute | solution.py:43
  13.2 1.1 %collective-permute-start.3 = (bf16[17,128,128]{2,1,0:T(8,128)(2,1)S(1)}, bf16[17,128,128]{2,1,0:T(8,128)(2,1)S(1)}, u32[]{:S(2)}, u32[]{:S(2)}) collective-permute-start(bf16[17,128,128]{2,1,0:T(8,128)(2,1)S(1)} %note.1.p_ref.own_ref.own), channel_id=1, source_target_pairs={{2,1},{3,0},{1,2},{0,3},{4,7},{5,6},{7,4},{6,5},{10,9},{11,8},{9,1... | collective-permute-start | bytes 1671176 | tf_op jit(solution)/shard_map/ppermute | solution.py:43
  14.3 2.1 %collective-permute-start.4 = (bf16[17,128,128]{2,1,0:T(8,128)(2,1)S(1)}, bf16[17,128,128]{2,1,0:T(8,128)(2,1)S(1)}, u32[]{:S(2)}, u32[]{:S(2)}) collective-permute-start(bf16[17,128,128]{2,1,0:T(8,128)(2,1)S(1)} %note.1.p_ref.own_ref.own), channel_id=1, source_target_pairs={{2,0},{3,1},{1,3},{0,2},{4,6},{5,7},{7,5},{6,4},{10,8},{11,9},{9,1... | collective-permute-start | bytes 1671176 | tf_op jit(solution)/shard_map/ppermute | solution.py:43
  16.4 0.0 collective-permute-done.near_ref
  16.4 0.0 collective-permute-done.1.far_ref
  16.4 0.0 copy-start.3
  16.4 0.7 %copy-done.3 = s32[16,1]{0,1:T(1,128)S(1)} copy-done((s32[16,1]{0,1:T(1,128)S(1)}, s32[16,1]{0,1:T(1,128)}, u32[]{:S(2)}) %copy-start.3) | copy-done | bytes 88
  17.1 0.0 copy-start.4
  17.1 0.7 %copy-done.4 = s32[16,27]{1,0:T(8,128)S(1)} copy-done((s32[16,27]{1,0:T(8,128)S(1)}, s32[16,27]{1,0:T(8,128)}, u32[]{:S(2)}) %copy-start.4) | copy-done | bytes 1752
  17.8 13.6 %products.1.sums_ref = bf16[16,384,128]{2,1,0:T(8,128)(2,1)S(1)} custom-call(s32[16,27]{1,0:T(8,128)S(1)} %copy-done.4, s32[16]{0:T(128)S(1)} %bitcast.4, bf16[16,27,128,128]{3,2,1,0:T(8,128)(2,1)} %a_ref.1, bf16[17,128,128]{2,1,0:T(8,128)(2,1)S(1)} %note.1.p_ref.own_ref.own, bf16[3,128,128]{2,1,0:T(8,128)(2,1)S(1)} %collective-permute-done.near_ref, ...), custom_call_target="tpu_custom_call" | custom-call | flops 7000000000 | bytes 15000000 | tf_op jit(solution)/shard_map/products/pallas_call | solution.py:236
  31.4 0.0 collective-permute-done.2.swapped
  31.4 2.8 %collective-permute-done.3.across = bf16[17,128,128]{2,1,0:T(8,128)(2,1)S(1)} collective-permute-done((bf16[17,128,128]{2,1,0:T(8,128)(2,1)S(1)}, bf16[17,128,128]{2,1,0:T(8,128)(2,1)S(1)}, u32[]{:S(2)}, u32[]{:S(2)}) %collective-permute-start.3) | collective-permute-done | bytes 557088 | tf_op jit(solution)/shard_map/ppermute | solution.py:43
  34.3 0.0 collective-permute-done.4.crossed
  34.3 2.3 %partials.1 = (f32[2,384,128]{2,1,0:T(8,128)S(1)}, f32[2,384,128]{2,1,0:T(8,128)S(1)}) custom-call(bf16[16,384,128]{2,1,0:T(8,128)(2,1)S(1)} %products.1.sums_ref, bf16[17,128,128]{2,1,0:T(8,128)(2,1)S(1)} %note.1.p_ref.own_ref.own, bf16[17,128,128]{2,1,0:T(8,128)(2,1)S(1)} %collective-permute-done.2.swapped, ...), custom_call_target="tpu_custom_call" | custom-call | tf_op jit(solution)/shard_map/partials/pallas_call | solution.py:245
  36.6 0.1 collective-permute-start.5
  36.7 6.8 %collective-permute-start.6 = (f32[2,384,128]{2,1,0:T(8,128)S(1)}, f32[2,384,128]{2,1,0:T(8,128)S(1)}, u32[]{:S(2)}, u32[]{:S(2)}) collective-permute-start(f32[2,384,128]{2,1,0:T(8,128)S(1)} %get-tuple-element.15), channel_id=1, source_target_pairs={{0,252},{4,8},{8,4},{12,16},{16,12},{20,24},{24,20},{28,32},{32,28... | collective-permute-start | bytes 1179656 | tf_op jit(solution)/shard_map/ppermute | solution.py:48
  43.5 2.3 %local.1 = (f32[2,32,128,128]{3,2,1,0:T(8,128)}, f32[2,512,128]{2,1,0:T(8,128)S(1)}) custom-call(bf16[16,384,128]{2,1,0:T(8,128)(2,1)S(1)} %products.1.sums_ref, bf16[17,128,128]{2,1,0:T(8,128)(2,1)S(1)} %note.1.p_ref.own_ref.own, bf16[17,128,128]{2,1,0:T(8,128)(2,1)S(1)} %collective-permute-done.2.swapped, ...), custom_call_target="tpu_custom_call" | custom-call | tf_op jit(solution)/shard_map/local/pallas_call | solution.py:253
  45.8 0.0 collective-permute-done.5.near_ref
  45.8 3.1 %collective-permute-done.6.far_ref = f32[2,384,128]{2,1,0:T(8,128)S(1)} collective-permute-done((f32[2,384,128]{2,1,0:T(8,128)S(1)}, f32[2,384,128]{2,1,0:T(8,128)S(1)}, u32[]{:S(2)}, u32[]{:S(2)}) %collective-permute-start.6) | collective-permute-done | bytes 393248 | tf_op jit(solution)/shard_map/ppermute | solution.py:48
  48.9 1.0 %final.1 = f32[2,32,128,128]{3,2,1,0:T(8,128)} custom-call(f32[2,512,128]{2,1,0:T(8,128)S(1)} %get-tuple-element.14.total_ref, f32[2,384,128]{2,1,0:T(8,128)S(1)} %collective-permute-done.5.near_ref, f32[2,384,128]{2,1,0:T(8,128)S(1)} %collective-permute-done.6.far_ref, f32[2,32,128,128]{3,2,1,0:T(8,128)} %get-tuple-element.16.zeroed), custom_call_target="tpu_custom_call", output_to_operand_aliasing={{}: (3, {})} | custom-call | tf_op jit(solution)/shard_map/final/pallas_call | solution.py:260
Async XLA Ops:
  0.0 1.0 %copy-start = (bf16[16,1,128,128]{3,2,1,0:T(8,128)(2,1)S(1)}, bf16[16,1,128,128]{3,2,1,0:T(8,128)(2,1)}, u32[]{:S(2)}) copy-start(bf16[16,1,128,128]{3,2,1,0:T(8,128)(2,1)} %param.7) | copy-start | bytes 1572868
  1.0 0.7 %copy-start.2 = (s32[16,1]{0,1:T(1,128)S(1)}, s32[16,1]{0,1:T(1,128)}, u32[]{:S(2)}) copy-start(s32[16,1]{0,1:T(1,128)} %param.8) | copy-start | bytes 196
  2.3 0.7 %copy-start.1 = (s32[2,2]{1,0:T(2,128)S(1)}, s32[2,2]{1,0:T(2,128)}, u32[]{:S(2)}) copy-start(s32[2,2]{1,0:T(2,128)} %send_ref.1) | copy-start | bytes 52
  3.8 12.6 %collective-permute-start = (bf16[3,128,128]{2,1,0:T(8,128)(2,1)S(1)}, bf16[3,128,128]{2,1,0:T(8,128)(2,1)S(1)}, u32[]{:S(2)}, u32[]{:S(2)}) collective-permute-start(bf16[3,128,128]{2,1,0:T(8,128)(2,1)S(1)} %get-tuple-element.11), channel_id=1, source_target_pairs={{0,4},{4,0},{8,12},{12,8},{16,20},{20,16},{24,28},{28,24},{32,36},... | collective-permute-start | bytes 294920 | tf_op jit(solution)/shard_map/ppermute | solution.py:48
  3.9 12.5 %collective-permute-start.1 = (bf16[3,128,128]{2,1,0:T(8,128)(2,1)S(1)}, bf16[3,128,128]{2,1,0:T(8,128)(2,1)S(1)}, u32[]{:S(2)}, u32[]{:S(2)}) collective-permute-start(bf16[3,128,128]{2,1,0:T(8,128)(2,1)S(1)} %get-tuple-element.12), channel_id=1, source_target_pairs={{0,252},{4,8},{8,4},{12,16},{16,12},{20,24},{24,20},{28,32},{32,28... | collective-permute-start | bytes 294920 | tf_op jit(solution)/shard_map/ppermute | solution.py:48
  12.3 19.1 %collective-permute-start.2 = (bf16[17,128,128]{2,1,0:T(8,128)(2,1)S(1)}, bf16[17,128,128]{2,1,0:T(8,128)(2,1)S(1)}, u32[]{:S(2)}, u32[]{:S(2)}) collective-permute-start(bf16[17,128,128]{2,1,0:T(8,128)(2,1)S(1)} %note.1.p_ref.own_ref.own), channel_id=1, source_target_pairs={{2,3},{3,2},{1,0},{0,1},{4,5},{5,4},{7,6},{6,7},{10,11},{11,10},{9... | collective-permute-start | bytes 1671176 | tf_op jit(solution)/shard_map/ppermute | solution.py:43
  13.2 21.1 %collective-permute-start.3 = (bf16[17,128,128]{2,1,0:T(8,128)(2,1)S(1)}, bf16[17,128,128]{2,1,0:T(8,128)(2,1)S(1)}, u32[]{:S(2)}, u32[]{:S(2)}) collective-permute-start(bf16[17,128,128]{2,1,0:T(8,128)(2,1)S(1)} %note.1.p_ref.own_ref.own), channel_id=1, source_target_pairs={{2,1},{3,0},{1,2},{0,3},{4,7},{5,6},{7,4},{6,5},{10,9},{11,8},{9,1... | collective-permute-start | bytes 1671176 | tf_op jit(solution)/shard_map/ppermute | solution.py:43
  14.3 20.0 %collective-permute-start.4 = (bf16[17,128,128]{2,1,0:T(8,128)(2,1)S(1)}, bf16[17,128,128]{2,1,0:T(8,128)(2,1)S(1)}, u32[]{:S(2)}, u32[]{:S(2)}) collective-permute-start(bf16[17,128,128]{2,1,0:T(8,128)(2,1)S(1)} %note.1.p_ref.own_ref.own), channel_id=1, source_target_pairs={{2,0},{3,1},{1,3},{0,2},{4,6},{5,7},{7,5},{6,4},{10,8},{11,9},{9,1... | collective-permute-start | bytes 1671176 | tf_op jit(solution)/shard_map/ppermute | solution.py:43
  16.4 0.7 %copy-start.3 = (s32[16,1]{0,1:T(1,128)S(1)}, s32[16,1]{0,1:T(1,128)}, u32[]{:S(2)}) copy-start(s32[16,1]{0,1:T(1,128)} %param.8) | copy-start | bytes 196
  17.1 0.7 %copy-start.4 = (s32[16,27]{1,0:T(8,128)S(1)}, s32[16,27]{1,0:T(8,128)}, u32[]{:S(2)}) copy-start(s32[16,27]{1,0:T(8,128)} %cols_ref.1) | copy-start | bytes 5188
  36.6 9.2 %collective-permute-start.5 = (f32[2,384,128]{2,1,0:T(8,128)S(1)}, f32[2,384,128]{2,1,0:T(8,128)S(1)}, u32[]{:S(2)}, u32[]{:S(2)}) collective-permute-start(f32[2,384,128]{2,1,0:T(8,128)S(1)} %get-tuple-element.13.after), channel_id=1, source_target_pairs={{0,4},{4,0},{8,12},{12,8},{16,20},{20,16},{24,28},{28,24},{32,36},... | collective-permute-start | bytes 1179656 | tf_op jit(solution)/shard_map/ppermute | solution.py:48
  36.7 12.2 %collective-permute-start.6 = (f32[2,384,128]{2,1,0:T(8,128)S(1)}, f32[2,384,128]{2,1,0:T(8,128)S(1)}, u32[]{:S(2)}, u32[]{:S(2)}) collective-permute-start(f32[2,384,128]{2,1,0:T(8,128)S(1)} %get-tuple-element.15), channel_id=1, source_target_pairs={{0,252},{4,8},{8,4},{12,16},{16,12},{20,24},{24,20},{28,32},{32,28... | collective-permute-start | bytes 1179656 | tf_op jit(solution)/shard_map/ppermute | solution.py:48
where the time goes:
time: 50.1 us; the launch traced here: 49.9 us
  Pallas kernels  20.6 us (41%)
  starting transfers between devices  19.5 us (39%)
  waiting for transfers between devices  5.97 us (12%)
  local copies, waits for them, and re-layouts  3.72 us (7%)
    ppermute x4, starting transfers between devices, swap_rows(): return lax.ppermute(block, 'row', pairs)  15.4 us
    pallas_call x1, Pallas kernels, shards(): pl.pallas_call(product_kernel, out_shape=jax.ShapeDtypeStruct((BR, G * T,...  13.6 us
    ppermute x3, starting transfers between devices, send(): return lax.ppermute(block, ('row', 'col'), pairs)  4.09 us
    unnamed x10, local copies, waits for them, and re-layouts  3.72 us
    ppermute x4, waiting for transfers between devices, swap_rows(): return lax.ppermute(block, 'row', pairs)  3.12 us
    ppermute x3, waiting for transfers between devices, send(): return lax.ppermute(block, ('row', 'col'), pairs)  2.85 us
    pallas_call x1, Pallas kernels, shards(): pl.pallas_call(local_kernel, out_shape=(out, jax.ShapeDtypeStruct((2, 4 *...  2.33 us
    pallas_call x1, Pallas kernels, shards(): pl.pallas_call(partial_kernel, out_shape=(travels, travels), in_specs=[VM...  2.3 us
  transfers between devices with their start and end apart: 7, of which 2 were waited for; matrix products, arithmetic and copies ran while one was open for 0% of the time, Pallas kernels for 32%

commit v1 on v0

--- a/solution.py
+++ b/solution.py
@@ -74,7 +74,7 @@
         copy.wait()
 
 
-def product_kernel(cols_ref, ids_ref, a_ref, own_ref, near_ref, far_ref, sums_ref, tiles, right, own, ghosts, sems):
+def product_kernel(cols_ref, ids_ref, a_ref, own_ref, near_ref, far_ref, sums_ref, rest_ref, tiles, right, own, ghosts, sems):
     early = [pltpu.make_async_copy(own_ref.at[pl.ds(0, BR)], own, sems.at[BR]),
              pltpu.make_async_copy(near_ref, ghosts.at[0], sems.at[BR + 1]),
              pltpu.make_async_copy(far_ref, ghosts.at[1], sems.at[BR + 2])]
@@ -107,7 +107,9 @@
             [jnp.concatenate([right[j + g] for g in range(G)], axis=1) for j in rows], axis=0)
         acc = jnp.dot(left, both, preferred_element_type=F32)
         turned = jnp.concatenate([acc[:, g * T:(g + 1) * T].T for g in range(G)], axis=0)
-        sums_ref[i] = turned.astype(BF16)
+        high = turned.astype(BF16)
+        sums_ref[i] = high
+        rest_ref[i] = (turned - high.astype(F32)).astype(BF16)
 
     def step(n, _):
         for k in range(UNROLL):
@@ -147,11 +149,11 @@
             masked[n, i * T:(i + 1) * T, :T] = jnp.where(lower, tile, 0.0).astype(BF16)
             masked[n, i * T:(i + 1) * T, T:] = jnp.where(lower, 0.0, tile).astype(BF16)
         terms = jnp.dot(sums, masked[n], preferred_element_type=F32)
-        near_ref[row] = jnp.where(odd, terms[:, :T], terms[:, T:])
-        far_ref[row] = jnp.where(odd, terms[:, T:], terms[:, :T])
-
-
-def local_kernel(sums_ref, own, swapped, across, crossed, after, out_ref, total_ref, tiles, zeros, sems):
+        near_ref[row] = jnp.where(odd, terms[:, :T], terms[:, T:]).astype(BF16)
+        far_ref[row] = jnp.where(odd, terms[:, T:], terms[:, :T]).astype(BF16)
+
+
+def local_kernel(sums_ref, rest_ref, own, swapped, across, crossed, after, out_ref, total_ref, tiles, zeros, sems):
     del after
     s, is_n, number, first = place()
 
@@ -178,7 +180,8 @@
         pltpu.make_async_copy(own, tiles.at[n], sems.at[n]).wait()
         right = tiles[n, :BR].reshape(BR * T, T)
         row = first_row if n == 0 else 1 - first_row
-        total_ref[row, at, :] = jnp.dot(sums, right, preferred_element_type=F32)
+        total_ref[row, at, :] = (jnp.dot(sums, right, preferred_element_type=F32)
+                                 + jnp.dot(wide(rest_ref), right, preferred_element_type=F32))
     for copy in copies:
         copy.wait()
 
@@ -194,10 +197,10 @@
             block = total_ref[r, q * T:(q + 1) * T, :]
             if q < G:
                 at = slice(q * T, (q + 1) * T)
-                block += jnp.where(odd, near_ref[r, at, :], far_ref[r, at, :])
+                block += jnp.where(odd, near_ref[r, at, :].astype(F32), far_ref[r, at, :].astype(F32))
             if q > 0:
                 at = slice((q - 1) * T, q * T)
-                block += jnp.where(odd, far_ref[r, at, :], near_ref[r, at, :])
+                block += jnp.where(odd, far_ref[r, at, :].astype(F32), near_ref[r, at, :].astype(F32))
             blocks[r, q] = block.T
             column = lax.rem(base + 4 * q + T, T) // 4
             copy = pltpu.make_async_copy(blocks.at[r, q], out_ref.at[r, column], sems.at[r * 4 + q])
@@ -226,22 +229,22 @@
     swapped = go(noted, ((N1, N2), (N2, N1), (L1, L2), (L2, L1)))
     across = go(noted, ((N1, L1), (N2, L2), (L1, N1), (L2, N2)))
     crossed = go(noted, ((N1, L2), (N2, L1), (L1, N2), (L2, N1)))
-    swapped_late, across_late, crossed_late = swapped, across, crossed
     ghost = jax.ShapeDtypeStruct((3, T, T), BF16)
     near, far = pl.pallas_call(
         pick_kernel, out_shape=(ghost, ghost), in_specs=[SMEM, HBM], out_specs=(VMEM, VMEM),
         scratch_shapes=[pltpu.SemaphoreType.DMA((8,))], compiler_params=params(8), name="pick",
     )(send_rows, noted)
     near, far = swap_rows(near, 0, rows, cols), swap_rows(far, 1, rows, cols)
-    sums = pl.pallas_call(
-        product_kernel, out_shape=jax.ShapeDtypeStruct((BR, G * T, T), BF16),
-        in_specs=[SMEM, SMEM, FIXED, HBM, HBM, HBM], out_specs=VMEM,
+    turned = jax.ShapeDtypeStruct((BR, G * T, T), BF16)
+    sums, rest = pl.pallas_call(
+        product_kernel, out_shape=(turned, turned),
+        in_specs=[SMEM, SMEM, FIXED, HBM, HBM, HBM], out_specs=(VMEM, VMEM),
         scratch_shapes=[pltpu.VMEM((BR, KA, T, T), BF16), pltpu.VMEM(((BR + 4) * G, T, T), BF16),
                         pltpu.VMEM((BR, T, T), BF16), pltpu.VMEM((2, 3, T, T), BF16),
                         pltpu.SemaphoreType.DMA((BR + 3,))],
-        compiler_params=params(50), cost_estimate=cost(7_000_000_000, 15_000_000), name="products",
+        compiler_params=params(50), name="products",
     )(a_cols, ids, a_tiles, noted, near, far)
-    travels = jax.ShapeDtypeStruct((2, G * T, T), F32)
+    travels = jax.ShapeDtypeStruct((2, G * T, T), BF16)
     near, far = pl.pallas_call(
         partial_kernel, out_shape=(travels, travels), in_specs=[VMEM] + [HBM] * 4, out_specs=(VMEM, VMEM),
         scratch_shapes=[pltpu.VMEM((2, BR + 1, T, T), BF16), pltpu.VMEM((2, BR * T, 2 * T), BF16),
@@ -252,11 +255,11 @@
     out = jax.ShapeDtypeStruct((2, NCC, T, T), F32)
     zeroed, total = pl.pallas_call(
         local_kernel, out_shape=(out, jax.ShapeDtypeStruct((2, 4 * T, T), F32)),
-        in_specs=[VMEM] + [HBM] * 5, out_specs=(HBM, VMEM),
+        in_specs=[VMEM] * 2 + [HBM] * 5, out_specs=(HBM, VMEM),
         scratch_shapes=[pltpu.VMEM((2, BR + 1, T, T), BF16), pltpu.VMEM((8, T, T), F32),
                         pltpu.SemaphoreType.DMA((10,))],
         compiler_params=params(24), name="local",
-    )(sums, noted, swapped_late, across_late, crossed_late, near)
+    )(sums, rest, noted, swapped, across, crossed, near)
     return pl.pallas_call(
         final_kernel, out_shape=out, in_specs=[VMEM] * 3 + [HBM], out_specs=HBM,
         scratch_shapes=[pltpu.VMEM((2, 4, T, T), F32), pltpu.SemaphoreType.DMA((8,))],

time: 50.1 us -> 48.6 us (0.970)
  the two profiles are of different devices: /device:TPU:6 before, /device:TPU:1 now
where the time goes in v1:
time: 48.6 us; the launch traced here: 48.4 us
  Pallas kernels  22.8 us (47%)
  starting transfers between devices  17.6 us (36%)
  waiting for transfers between devices  4.17 us (9%)
  local copies, waits for them, and re-layouts  3.73 us (8%)
    pallas_call x1, Pallas kernels, shards(): pl.pallas_call(product_kernel, out_shape=(turned, turned), in_specs=[SMEM...  14.2 us
    ppermute x4, starting transfers between devices, swap_rows(): return lax.ppermute(block, 'row', pairs)  13.1 us
    ppermute x3, starting transfers between devices, send(): return lax.ppermute(block, ('row', 'col'), pairs)  4.52 us
    pallas_call x1, Pallas kernels, shards(): pl.pallas_call(local_kernel, out_shape=(out, jax.ShapeDtypeStruct((2, 4 *...  3.95 us
    ppermute x4, waiting for transfers between devices, swap_rows(): return lax.ppermute(block, 'row', pairs)  3.78 us
    unnamed x10, local copies, waits for them, and re-layouts  3.73 us
    pallas_call x1, Pallas kernels, shards(): pl.pallas_call(partial_kernel, out_shape=(travels, travels), in_specs=[VM...  2.31 us
  transfers between devices with their start and end apart: 7, of which 3 were waited for; matrix products, arithmetic and copies ran while one was open for 0% of the time, Pallas kernels for 39%

profile of v1, /device:TPU:1, one launch (start us, length us, event | category | flops | bytes accessed | tf_op | source)
XLA Modules:
  0.0 48.4 jit_solution(2951243863971097970)
XLA Ops:
  0.0 0.0 copy-start
  0.0 1.0 %copy-done = bf16[16,1,128,128]{3,2,1,0:T(8,128)(2,1)S(1)} copy-done((bf16[16,1,128,128]{3,2,1,0:T(8,128)(2,1)S(1)}, bf16[16,1,128,128]{3,2,1,0:T(8,128)(2,1)}, u32[]{:S(2)}) %copy-start) | copy-done | bytes 524312
  1.0 0.0 copy-start.2
  1.0 0.7 %copy-done.2 = s32[16,1]{0,1:T(1,128)S(1)} copy-done((s32[16,1]{0,1:T(1,128)S(1)}, s32[16,1]{0,1:T(1,128)}, u32[]{:S(2)}) %copy-start.2) | copy-done | bytes 88
  1.7 0.6 %note.1.p_ref.own_ref.own = bf16[17,128,128]{2,1,0:T(8,128)(2,1)S(1)} custom-call(s32[16]{0:T(128)S(1)} %bitcast.3, bf16[16,128,128]{2,1,0:T(8,128)(2,1)S(1)} %bitcast.2), custom_call_target="tpu_custom_call" | custom-call | tf_op jit(solution)/shard_map/note/pallas_call | solution.py:225
  2.3 3.7 %collective-permute-start.4 = (bf16[17,128,128]{2,1,0:T(8,128)(2,1)S(1)}, bf16[17,128,128]{2,1,0:T(8,128)(2,1)S(1)}, u32[]{:S(2)}, u32[]{:S(2)}) collective-permute-start(bf16[17,128,128]{2,1,0:T(8,128)(2,1)S(1)} %note.1.p_ref.own_ref.own), channel_id=1, source_target_pairs={{2,0},{3,1},{1,3},{0,2},{4,6},{5,7},{7,5},{6,4},{10,8},{11,9},{9,1... | collective-permute-start | bytes 1671176 | tf_op jit(solution)/shard_map/ppermute | solution.py:43
  6.0 0.9 %collective-permute-start.3 = (bf16[17,128,128]{2,1,0:T(8,128)(2,1)S(1)}, bf16[17,128,128]{2,1,0:T(8,128)(2,1)S(1)}, u32[]{:S(2)}, u32[]{:S(2)}) collective-permute-start(bf16[17,128,128]{2,1,0:T(8,128)(2,1)S(1)} %note.1.p_ref.own_ref.own), channel_id=1, source_target_pairs={{2,1},{3,0},{1,2},{0,3},{4,7},{5,6},{7,4},{6,5},{10,9},{11,8},{9,1... | collective-permute-start | bytes 1671176 | tf_op jit(solution)/shard_map/ppermute | solution.py:43
  6.8 0.0 collective-permute-start.2
  6.8 0.0 copy-start.4
  6.8 0.7 %copy-done.4 = s32[2,2]{1,0:T(2,128)S(1)} copy-done((s32[2,2]{1,0:T(2,128)S(1)}, s32[2,2]{1,0:T(2,128)}, u32[]{:S(2)}) %copy-start.4) | copy-done | bytes 40
  7.5 0.8 %pick.1 = (bf16[3,128,128]{2,1,0:T(8,128)(2,1)S(1)}, bf16[3,128,128]{2,1,0:T(8,128)(2,1)S(1)}) custom-call(s32[2,2]{1,0:T(2,128)S(1)} %copy-done.4, bf16[17,128,128]{2,1,0:T(8,128)(2,1)S(1)} %note.1.p_ref.own_ref.own), custom_call_target="tpu_custom_call" | custom-call | tf_op jit(solution)/shard_map/pick/pallas_call | solution.py:233
  8.3 2.4 %collective-permute-start = (bf16[3,128,128]{2,1,0:T(8,128)(2,1)S(1)}, bf16[3,128,128]{2,1,0:T(8,128)(2,1)S(1)}, u32[]{:S(2)}, u32[]{:S(2)}) collective-permute-start(bf16[3,128,128]{2,1,0:T(8,128)(2,1)S(1)} %get-tuple-element.13), channel_id=1, source_target_pairs={{0,4},{4,0},{8,12},{12,8},{16,20},{20,16},{24,28},{28,24},{32,36},... | collective-permute-start | bytes 294920 | tf_op jit(solution)/shard_map/ppermute | solution.py:48
  10.7 0.6 %collective-permute-start.1 = (bf16[3,128,128]{2,1,0:T(8,128)(2,1)S(1)}, bf16[3,128,128]{2,1,0:T(8,128)(2,1)S(1)}, u32[]{:S(2)}, u32[]{:S(2)}) collective-permute-start(bf16[3,128,128]{2,1,0:T(8,128)(2,1)S(1)} %get-tuple-element.14), channel_id=1, source_target_pairs={{0,252},{4,8},{8,4},{12,16},{16,12},{20,24},{24,20},{28,32},{32,28... | collective-permute-start | bytes 294920 | tf_op jit(solution)/shard_map/ppermute | solution.py:48
  11.3 0.4 collective-permute-done.near_ref
  11.7 3.4 %collective-permute-done.1.far_ref = bf16[3,128,128]{2,1,0:T(8,128)(2,1)S(1)} collective-permute-done((bf16[3,128,128]{2,1,0:T(8,128)(2,1)S(1)}, bf16[3,128,128]{2,1,0:T(8,128)(2,1)S(1)}, u32[]{:S(2)}, u32[]{:S(2)}) %collective-permute-start.1) | collective-permute-done | bytes 98336 | tf_op jit(solution)/shard_map/ppermute | solution.py:48
  15.1 0.0 copy-start.1
  15.1 0.7 %copy-done.1 = s32[16,27]{1,0:T(8,128)S(1)} copy-done((s32[16,27]{1,0:T(8,128)S(1)}, s32[16,27]{1,0:T(8,128)}, u32[]{:S(2)}) %copy-start.1) | copy-done | bytes 1752
  15.8 0.0 copy-start.3
  15.8 0.7 %copy-done.3 = s32[16,1]{0,1:T(1,128)S(1)} copy-done((s32[16,1]{0,1:T(1,128)S(1)}, s32[16,1]{0,1:T(1,128)}, u32[]{:S(2)}) %copy-start.3) | copy-done | bytes 88
  16.4 14.2 %products.1 = (bf16[16,384,128]{2,1,0:T(8,128)(2,1)S(1)}, bf16[16,384,128]{2,1,0:T(8,128)(2,1)S(1)}) custom-call(s32[16,27]{1,0:T(8,128)S(1)} %copy-done.1, s32[16]{0:T(128)S(1)} %bitcast.4, bf16[16,27,128,128]{3,2,1,0:T(8,128)(2,1)} %a_ref.1, bf16[17,128,128]{2,1,0:T(8,128)(2,1)S(1)} %note.1.p_ref.own_ref.own, ...), custom_call_target="tpu_custom_call" | custom-call | tf_op jit(solution)/shard_map/products/pallas_call | solution.py:239
  30.6 0.0 collective-permute-done.4.crossed
  30.6 0.4 collective-permute-done.3.across
  31.0 0.0 collective-permute-done.2.swapped
  31.0 2.3 %partials.1 = (bf16[2,384,128]{2,1,0:T(8,128)(2,1)S(1)}, bf16[2,384,128]{2,1,0:T(8,128)(2,1)S(1)}) custom-call(bf16[16,384,128]{2,1,0:T(8,128)(2,1)S(1)} %get-tuple-element.15.sums_ref, bf16[17,128,128]{2,1,0:T(8,128)(2,1)S(1)} %note.1.p_ref.own_ref.own, bf16[17,128,128]{2,1,0:T(8,128)(2,1)S(1)} %collective-permute-done.2.swapped, ...), custom_call_target="tpu_custom_call" | custom-call | tf_op jit(solution)/shard_map/partials/pallas_call | solution.py:248
  33.3 2.4 %collective-permute-start.6 = (bf16[2,384,128]{2,1,0:T(8,128)(2,1)S(1)}, bf16[2,384,128]{2,1,0:T(8,128)(2,1)S(1)}, u32[]{:S(2)}, u32[]{:S(2)}) collective-permute-start(bf16[2,384,128]{2,1,0:T(8,128)(2,1)S(1)} %get-tuple-element.19), channel_id=1, source_target_pairs={{0,252},{4,8},{8,4},{12,16},{16,12},{20,24},{24,20},{28,32},{32,28... | collective-permute-start | bytes 589832 | tf_op jit(solution)/shard_map/ppermute | solution.py:48
  35.8 7.7 %collective-permute-start.5 = (bf16[2,384,128]{2,1,0:T(8,128)(2,1)S(1)}, bf16[2,384,128]{2,1,0:T(8,128)(2,1)S(1)}, u32[]{:S(2)}, u32[]{:S(2)}) collective-permute-start(bf16[2,384,128]{2,1,0:T(8,128)(2,1)S(1)} %get-tuple-element.17.after), channel_id=1, source_target_pairs={{0,4},{4,0},{8,12},{12,8},{16,20},{20,16},{24,28},{28,24},{32,36},... | collective-permute-start | bytes 589832 | tf_op jit(solution)/shard_map/ppermute | solution.py:48
  43.4 3.9 %local.1 = (f32[2,32,128,128]{3,2,1,0:T(8,128)}, f32[2,512,128]{2,1,0:T(8,128)S(1)}) custom-call(bf16[16,384,128]{2,1,0:T(8,128)(2,1)S(1)} %get-tuple-element.15.sums_ref, bf16[16,384,128]{2,1,0:T(8,128)(2,1)S(1)} %get-tuple-element.16.rest_ref, bf16[17,128,128]{2,1,0:T(8,128)(2,1)S(1)} %note.1.p_ref.own_ref.own, ...), custom_call_target="tpu_custom_call" | custom-call | tf_op jit(solution)/shard_map/local/pallas_call | solution.py:256
  47.4 0.0 collective-permute-done.6.far_ref
  47.4 0.0 collective-permute-done.5.near_ref
  47.4 1.0 %final.1 = f32[2,32,128,128]{3,2,1,0:T(8,128)} custom-call(f32[2,512,128]{2,1,0:T(8,128)S(1)} %get-tuple-element.18.total_ref, bf16[2,384,128]{2,1,0:T(8,128)(2,1)S(1)} %collective-permute-done.5.near_ref, bf16[2,384,128]{2,1,0:T(8,128)(2,1)S(1)} %collective-permute-done.6.far_ref, ...), custom_call_target="tpu_custom_call", output_to_operand_aliasing={{}: (3, {})} | custom-call | tf_op jit(solution)/shard_map/final/pallas_call | solution.py:263
Async XLA Ops:
  0.0 1.0 %copy-start = (bf16[16,1,128,128]{3,2,1,0:T(8,128)(2,1)S(1)}, bf16[16,1,128,128]{3,2,1,0:T(8,128)(2,1)}, u32[]{:S(2)}) copy-start(bf16[16,1,128,128]{3,2,1,0:T(8,128)(2,1)} %param.7) | copy-start | bytes 1572868
  1.0 0.7 %copy-start.2 = (s32[16,1]{0,1:T(1,128)S(1)}, s32[16,1]{0,1:T(1,128)}, u32[]{:S(2)}) copy-start(s32[16,1]{0,1:T(1,128)} %param.8) | copy-start | bytes 196
  2.3 28.3 %collective-permute-start.4 = (bf16[17,128,128]{2,1,0:T(8,128)(2,1)S(1)}, bf16[17,128,128]{2,1,0:T(8,128)(2,1)S(1)}, u32[]{:S(2)}, u32[]{:S(2)}) collective-permute-start(bf16[17,128,128]{2,1,0:T(8,128)(2,1)S(1)} %note.1.p_ref.own_ref.own), channel_id=1, source_target_pairs={{2,0},{3,1},{1,3},{0,2},{4,6},{5,7},{7,5},{6,4},{10,8},{11,9},{9,1... | collective-permute-start | bytes 1671176 | tf_op jit(solution)/shard_map/ppermute | solution.py:43
  6.0 25.0 %collective-permute-start.3 = (bf16[17,128,128]{2,1,0:T(8,128)(2,1)S(1)}, bf16[17,128,128]{2,1,0:T(8,128)(2,1)S(1)}, u32[]{:S(2)}, u32[]{:S(2)}) collective-permute-start(bf16[17,128,128]{2,1,0:T(8,128)(2,1)S(1)} %note.1.p_ref.own_ref.own), channel_id=1, source_target_pairs={{2,1},{3,0},{1,2},{0,3},{4,7},{5,6},{7,4},{6,5},{10,9},{11,8},{9,1... | collective-permute-start | bytes 1671176 | tf_op jit(solution)/shard_map/ppermute | solution.py:43
  6.8 24.2 %collective-permute-start.2 = (bf16[17,128,128]{2,1,0:T(8,128)(2,1)S(1)}, bf16[17,128,128]{2,1,0:T(8,128)(2,1)S(1)}, u32[]{:S(2)}, u32[]{:S(2)}) collective-permute-start(bf16[17,128,128]{2,1,0:T(8,128)(2,1)S(1)} %note.1.p_ref.own_ref.own), channel_id=1, source_target_pairs={{2,3},{3,2},{1,0},{0,1},{4,5},{5,4},{7,6},{6,7},{10,11},{11,10},{9... | collective-permute-start | bytes 1671176 | tf_op jit(solution)/shard_map/ppermute | solution.py:43
  6.8 0.7 %copy-start.4 = (s32[2,2]{1,0:T(2,128)S(1)}, s32[2,2]{1,0:T(2,128)}, u32[]{:S(2)}) copy-start(s32[2,2]{1,0:T(2,128)} %send_ref.1) | copy-start | bytes 52
  8.3 3.3 %collective-permute-start = (bf16[3,128,128]{2,1,0:T(8,128)(2,1)S(1)}, bf16[3,128,128]{2,1,0:T(8,128)(2,1)S(1)}, u32[]{:S(2)}, u32[]{:S(2)}) collective-permute-start(bf16[3,128,128]{2,1,0:T(8,128)(2,1)S(1)} %get-tuple-element.13), channel_id=1, source_target_pairs={{0,4},{4,0},{8,12},{12,8},{16,20},{20,16},{24,28},{28,24},{32,36},... | collective-permute-start | bytes 294920 | tf_op jit(solution)/shard_map/ppermute | solution.py:48
  10.7 4.3 %collective-permute-start.1 = (bf16[3,128,128]{2,1,0:T(8,128)(2,1)S(1)}, bf16[3,128,128]{2,1,0:T(8,128)(2,1)S(1)}, u32[]{:S(2)}, u32[]{:S(2)}) collective-permute-start(bf16[3,128,128]{2,1,0:T(8,128)(2,1)S(1)} %get-tuple-element.14), channel_id=1, source_target_pairs={{0,252},{4,8},{8,4},{12,16},{16,12},{20,24},{24,20},{28,32},{32,28... | collective-permute-start | bytes 294920 | tf_op jit(solution)/shard_map/ppermute | solution.py:48
  15.1 0.7 %copy-start.1 = (s32[16,27]{1,0:T(8,128)S(1)}, s32[16,27]{1,0:T(8,128)}, u32[]{:S(2)}) copy-start(s32[16,27]{1,0:T(8,128)} %cols_ref.1) | copy-start | bytes 5188
  15.8 0.7 %copy-start.3 = (s32[16,1]{0,1:T(1,128)S(1)}, s32[16,1]{0,1:T(1,128)}, u32[]{:S(2)}) copy-start(s32[16,1]{0,1:T(1,128)} %param.8) | copy-start | bytes 196
  33.3 14.1 %collective-permute-start.6 = (bf16[2,384,128]{2,1,0:T(8,128)(2,1)S(1)}, bf16[2,384,128]{2,1,0:T(8,128)(2,1)S(1)}, u32[]{:S(2)}, u32[]{:S(2)}) collective-permute-start(bf16[2,384,128]{2,1,0:T(8,128)(2,1)S(1)} %get-tuple-element.19), channel_id=1, source_target_pairs={{0,252},{4,8},{8,4},{12,16},{16,12},{20,24},{24,20},{28,32},{32,28... | collective-permute-start | bytes 589832 | tf_op jit(solution)/shard_map/ppermute | solution.py:48
  35.8 11.6 %collective-permute-start.5 = (bf16[2,384,128]{2,1,0:T(8,128)(2,1)S(1)}, bf16[2,384,128]{2,1,0:T(8,128)(2,1)S(1)}, u32[]{:S(2)}, u32[]{:S(2)}) collective-permute-start(bf16[2,384,128]{2,1,0:T(8,128)(2,1)S(1)} %get-tuple-element.17.after), channel_id=1, source_target_pairs={{0,4},{4,0},{8,12},{12,8},{16,20},{20,16},{24,28},{28,24},{32,36},... | collective-permute-start | bytes 589832 | tf_op jit(solution)/shard_map/ppermute | solution.py:48

commit v2 on v1

--- a/solution.py
+++ b/solution.py
@@ -178,10 +178,11 @@
     first_row = jnp.where(is_n, 1 - number, number)
     for n in range(2):
         pltpu.make_async_copy(own, tiles.at[n], sems.at[n]).wait()
-        right = tiles[n, :BR].reshape(BR * T, T)
-        row = first_row if n == 0 else 1 - first_row
-        total_ref[row, at, :] = (jnp.dot(sums, right, preferred_element_type=F32)
-                                 + jnp.dot(wide(rest_ref), right, preferred_element_type=F32))
+    right = jnp.concatenate([tiles[n, :BR].reshape(BR * T, T) for n in range(2)], axis=1)
+    terms = jnp.dot(sums, right, preferred_element_type=F32)
+    terms += jnp.dot(wide(rest_ref), right, preferred_element_type=F32)
+    total_ref[first_row, at, :] = terms[:, :T]
+    total_ref[1 - first_row, at, :] = terms[:, T:]
     for copy in copies:
         copy.wait()
 

time: 48.6 us -> 47 us (0.967)
  Pallas kernels: 22.8 us -> 21.1 us
    pallas_call x1, Pallas kernels: 3.95 us -> 2.27 us  [shards(): pl.pallas_call(local_kernel, out_shape=(out, jax.ShapeDtypeStruct((2, 4 *...]
  transfers between devices with their start and end apart: 7 -> 7, of which waited for: 3 -> 3; matrix products, arithmetic and copies ran while one was open for 0% -> 0% of each run, Pallas kernels for 39% -> 37%
where the time goes in v2:
time: 47 us; the launch traced here: 46.7 us
  Pallas kernels  21.1 us (45%)
  starting transfers between devices  17.6 us (37%)
  waiting for transfers between devices  4.17 us (9%)
  local copies, waits for them, and re-layouts  3.73 us (8%)
    pallas_call x1, Pallas kernels, shards(): pl.pallas_call(product_kernel, out_shape=(turned, turned), in_specs=[SMEM...  14.2 us
    ppermute x4, starting transfers between devices, swap_rows(): return lax.ppermute(block, 'row', pairs)  13.1 us
    ppermute x3, starting transfers between devices, send(): return lax.ppermute(block, ('row', 'col'), pairs)  4.52 us
    ppermute x4, waiting for transfers between devices, swap_rows(): return lax.ppermute(block, 'row', pairs)  3.78 us
    unnamed x10, local copies, waits for them, and re-layouts  3.73 us
    pallas_call x1, Pallas kernels, shards(): pl.pallas_call(partial_kernel, out_shape=(travels, travels), in_specs=[VM...  2.31 us
    pallas_call x1, Pallas kernels, shards(): pl.pallas_call(local_kernel, out_shape=(out, jax.ShapeDtypeStruct((2, 4 *...  2.27 us
    pallas_call x1, Pallas kernels, shards(): pl.pallas_call(final_kernel, out_shape=out, in_specs=[VMEM] * 3 + [HBM],...  0.97 us
  transfers between devices with their start and end apart: 7, of which 3 were waited for; matrix products, arithmetic and copies ran while one was open for 0% of the time, Pallas kernels for 37%

profile of v2, /device:TPU:1, one launch (start us, length us, event | category | flops | bytes accessed | tf_op | source)
XLA Modules:
  0.0 46.7 jit_solution(4448688402841862908)
XLA Ops:
  0.0 0.0 copy-start
  0.0 1.0 %copy-done = bf16[16,1,128,128]{3,2,1,0:T(8,128)(2,1)S(1)} copy-done((bf16[16,1,128,128]{3,2,1,0:T(8,128)(2,1)S(1)}, bf16[16,1,128,128]{3,2,1,0:T(8,128)(2,1)}, u32[]{:S(2)}) %copy-start) | copy-done | bytes 524312
  1.0 0.0 copy-start.2
  1.0 0.7 %copy-done.2 = s32[16,1]{0,1:T(1,128)S(1)} copy-done((s32[16,1]{0,1:T(1,128)S(1)}, s32[16,1]{0,1:T(1,128)}, u32[]{:S(2)}) %copy-start.2) | copy-done | bytes 88
  1.7 0.6 %note.1.p_ref.own_ref.own = bf16[17,128,128]{2,1,0:T(8,128)(2,1)S(1)} custom-call(s32[16]{0:T(128)S(1)} %bitcast.3, bf16[16,128,128]{2,1,0:T(8,128)(2,1)S(1)} %bitcast.2), custom_call_target="tpu_custom_call" | custom-call | tf_op jit(solution)/shard_map/note/pallas_call | solution.py:226
  2.3 3.7 %collective-permute-start.4 = (bf16[17,128,128]{2,1,0:T(8,128)(2,1)S(1)}, bf16[17,128,128]{2,1,0:T(8,128)(2,1)S(1)}, u32[]{:S(2)}, u32[]{:S(2)}) collective-permute-start(bf16[17,128,128]{2,1,0:T(8,128)(2,1)S(1)} %note.1.p_ref.own_ref.own), channel_id=1, source_target_pairs={{2,0},{3,1},{1,3},{0,2},{4,6},{5,7},{7,5},{6,4},{10,8},{11,9},{9,1... | collective-permute-start | bytes 1671176 | tf_op jit(solution)/shard_map/ppermute | solution.py:43
  6.0 0.9 %collective-permute-start.3 = (bf16[17,128,128]{2,1,0:T(8,128)(2,1)S(1)}, bf16[17,128,128]{2,1,0:T(8,128)(2,1)S(1)}, u32[]{:S(2)}, u32[]{:S(2)}) collective-permute-start(bf16[17,128,128]{2,1,0:T(8,128)(2,1)S(1)} %note.1.p_ref.own_ref.own), channel_id=1, source_target_pairs={{2,1},{3,0},{1,2},{0,3},{4,7},{5,6},{7,4},{6,5},{10,9},{11,8},{9,1... | collective-permute-start | bytes 1671176 | tf_op jit(solution)/shard_map/ppermute | solution.py:43
  6.8 0.0 collective-permute-start.2
  6.8 0.0 copy-start.4
  6.8 0.7 %copy-done.4 = s32[2,2]{1,0:T(2,128)S(1)} copy-done((s32[2,2]{1,0:T(2,128)S(1)}, s32[2,2]{1,0:T(2,128)}, u32[]{:S(2)}) %copy-start.4) | copy-done | bytes 40
  7.5 0.8 %pick.1 = (bf16[3,128,128]{2,1,0:T(8,128)(2,1)S(1)}, bf16[3,128,128]{2,1,0:T(8,128)(2,1)S(1)}) custom-call(s32[2,2]{1,0:T(2,128)S(1)} %copy-done.4, bf16[17,128,128]{2,1,0:T(8,128)(2,1)S(1)} %note.1.p_ref.own_ref.own), custom_call_target="tpu_custom_call" | custom-call | tf_op jit(solution)/shard_map/pick/pallas_call | solution.py:234
  8.3 2.4 %collective-permute-start = (bf16[3,128,128]{2,1,0:T(8,128)(2,1)S(1)}, bf16[3,128,128]{2,1,0:T(8,128)(2,1)S(1)}, u32[]{:S(2)}, u32[]{:S(2)}) collective-permute-start(bf16[3,128,128]{2,1,0:T(8,128)(2,1)S(1)} %get-tuple-element.13), channel_id=1, source_target_pairs={{0,4},{4,0},{8,12},{12,8},{16,20},{20,16},{24,28},{28,24},{32,36},... | collective-permute-start | bytes 294920 | tf_op jit(solution)/shard_map/ppermute | solution.py:48
  10.7 0.6 %collective-permute-start.1 = (bf16[3,128,128]{2,1,0:T(8,128)(2,1)S(1)}, bf16[3,128,128]{2,1,0:T(8,128)(2,1)S(1)}, u32[]{:S(2)}, u32[]{:S(2)}) collective-permute-start(bf16[3,128,128]{2,1,0:T(8,128)(2,1)S(1)} %get-tuple-element.14), channel_id=1, source_target_pairs={{0,252},{4,8},{8,4},{12,16},{16,12},{20,24},{24,20},{28,32},{32,28... | collective-permute-start | bytes 294920 | tf_op jit(solution)/shard_map/ppermute | solution.py:48
  11.3 0.4 collective-permute-done.near_ref
  11.7 3.4 %collective-permute-done.1.far_ref = bf16[3,128,128]{2,1,0:T(8,128)(2,1)S(1)} collective-permute-done((bf16[3,128,128]{2,1,0:T(8,128)(2,1)S(1)}, bf16[3,128,128]{2,1,0:T(8,128)(2,1)S(1)}, u32[]{:S(2)}, u32[]{:S(2)}) %collective-permute-start.1) | collective-permute-done | bytes 98336 | tf_op jit(solution)/shard_map/ppermute | solution.py:48
  15.1 0.0 copy-start.1
  15.1 0.7 %copy-done.1 = s32[16,27]{1,0:T(8,128)S(1)} copy-done((s32[16,27]{1,0:T(8,128)S(1)}, s32[16,27]{1,0:T(8,128)}, u32[]{:S(2)}) %copy-start.1) | copy-done | bytes 1752
  15.8 0.0 copy-start.3
  15.8 0.7 %copy-done.3 = s32[16,1]{0,1:T(1,128)S(1)} copy-done((s32[16,1]{0,1:T(1,128)S(1)}, s32[16,1]{0,1:T(1,128)}, u32[]{:S(2)}) %copy-start.3) | copy-done | bytes 88
  16.4 14.2 %products.1 = (bf16[16,384,128]{2,1,0:T(8,128)(2,1)S(1)}, bf16[16,384,128]{2,1,0:T(8,128)(2,1)S(1)}) custom-call(s32[16,27]{1,0:T(8,128)S(1)} %copy-done.1, s32[16]{0:T(128)S(1)} %bitcast.4, bf16[16,27,128,128]{3,2,1,0:T(8,128)(2,1)} %a_ref.1, bf16[17,128,128]{2,1,0:T(8,128)(2,1)S(1)} %note.1.p_ref.own_ref.own, ...), custom_call_target="tpu_custom_call" | custom-call | tf_op jit(solution)/shard_map/products/pallas_call | solution.py:240
  30.6 0.0 collective-permute-done.4.crossed
  30.6 0.4 collective-permute-done.3.across
  31.0 0.0 collective-permute-done.2.swapped
  31.0 2.3 %partials.1 = (bf16[2,384,128]{2,1,0:T(8,128)(2,1)S(1)}, bf16[2,384,128]{2,1,0:T(8,128)(2,1)S(1)}) custom-call(bf16[16,384,128]{2,1,0:T(8,128)(2,1)S(1)} %get-tuple-element.15.sums_ref, bf16[17,128,128]{2,1,0:T(8,128)(2,1)S(1)} %note.1.p_ref.own_ref.own, bf16[17,128,128]{2,1,0:T(8,128)(2,1)S(1)} %collective-permute-done.2.swapped, ...), custom_call_target="tpu_custom_call" | custom-call | tf_op jit(solution)/shard_map/partials/pallas_call | solution.py:249
  33.3 2.4 %collective-permute-start.6 = (bf16[2,384,128]{2,1,0:T(8,128)(2,1)S(1)}, bf16[2,384,128]{2,1,0:T(8,128)(2,1)S(1)}, u32[]{:S(2)}, u32[]{:S(2)}) collective-permute-start(bf16[2,384,128]{2,1,0:T(8,128)(2,1)S(1)} %get-tuple-element.19), channel_id=1, source_target_pairs={{0,252},{4,8},{8,4},{12,16},{16,12},{20,24},{24,20},{28,32},{32,28... | collective-permute-start | bytes 589832 | tf_op jit(solution)/shard_map/ppermute | solution.py:48
  35.8 7.7 %collective-permute-start.5 = (bf16[2,384,128]{2,1,0:T(8,128)(2,1)S(1)}, bf16[2,384,128]{2,1,0:T(8,128)(2,1)S(1)}, u32[]{:S(2)}, u32[]{:S(2)}) collective-permute-start(bf16[2,384,128]{2,1,0:T(8,128)(2,1)S(1)} %get-tuple-element.17.after), channel_id=1, source_target_pairs={{0,4},{4,0},{8,12},{12,8},{16,20},{20,16},{24,28},{28,24},{32,36},... | collective-permute-start | bytes 589832 | tf_op jit(solution)/shard_map/ppermute | solution.py:48
  43.4 2.3 %local.1 = (f32[2,32,128,128]{3,2,1,0:T(8,128)}, f32[2,512,128]{2,1,0:T(8,128)S(1)}) custom-call(bf16[16,384,128]{2,1,0:T(8,128)(2,1)S(1)} %get-tuple-element.15.sums_ref, bf16[16,384,128]{2,1,0:T(8,128)(2,1)S(1)} %get-tuple-element.16.rest_ref, bf16[17,128,128]{2,1,0:T(8,128)(2,1)S(1)} %note.1.p_ref.own_ref.own, ...), custom_call_target="tpu_custom_call" | custom-call | tf_op jit(solution)/shard_map/local/pallas_call | solution.py:257
  45.7 0.0 collective-permute-done.6.far_ref
  45.7 0.0 collective-permute-done.5.near_ref
  45.7 1.0 %final.1 = f32[2,32,128,128]{3,2,1,0:T(8,128)} custom-call(f32[2,512,128]{2,1,0:T(8,128)S(1)} %get-tuple-element.18.total_ref, bf16[2,384,128]{2,1,0:T(8,128)(2,1)S(1)} %collective-permute-done.5.near_ref, bf16[2,384,128]{2,1,0:T(8,128)(2,1)S(1)} %collective-permute-done.6.far_ref, ...), custom_call_target="tpu_custom_call", output_to_operand_aliasing={{}: (3, {})} | custom-call | tf_op jit(solution)/shard_map/final/pallas_call | solution.py:264
Async XLA Ops:
  0.0 1.0 %copy-start = (bf16[16,1,128,128]{3,2,1,0:T(8,128)(2,1)S(1)}, bf16[16,1,128,128]{3,2,1,0:T(8,128)(2,1)}, u32[]{:S(2)}) copy-start(bf16[16,1,128,128]{3,2,1,0:T(8,128)(2,1)} %param.7) | copy-start | bytes 1572868
  1.0 0.7 %copy-start.2 = (s32[16,1]{0,1:T(1,128)S(1)}, s32[16,1]{0,1:T(1,128)}, u32[]{:S(2)}) copy-start(s32[16,1]{0,1:T(1,128)} %param.8) | copy-start | bytes 196
  2.3 28.3 %collective-permute-start.4 = (bf16[17,128,128]{2,1,0:T(8,128)(2,1)S(1)}, bf16[17,128,128]{2,1,0:T(8,128)(2,1)S(1)}, u32[]{:S(2)}, u32[]{:S(2)}) collective-permute-start(bf16[17,128,128]{2,1,0:T(8,128)(2,1)S(1)} %note.1.p_ref.own_ref.own), channel_id=1, source_target_pairs={{2,0},{3,1},{1,3},{0,2},{4,6},{5,7},{7,5},{6,4},{10,8},{11,9},{9,1... | collective-permute-start | bytes 1671176 | tf_op jit(solution)/shard_map/ppermute | solution.py:43
  6.0 25.0 %collective-permute-start.3 = (bf16[17,128,128]{2,1,0:T(8,128)(2,1)S(1)}, bf16[17,128,128]{2,1,0:T(8,128)(2,1)S(1)}, u32[]{:S(2)}, u32[]{:S(2)}) collective-permute-start(bf16[17,128,128]{2,1,0:T(8,128)(2,1)S(1)} %note.1.p_ref.own_ref.own), channel_id=1, source_target_pairs={{2,1},{3,0},{1,2},{0,3},{4,7},{5,6},{7,4},{6,5},{10,9},{11,8},{9,1... | collective-permute-start | bytes 1671176 | tf_op jit(solution)/shard_map/ppermute | solution.py:43
  6.8 24.2 %collective-permute-start.2 = (bf16[17,128,128]{2,1,0:T(8,128)(2,1)S(1)}, bf16[17,128,128]{2,1,0:T(8,128)(2,1)S(1)}, u32[]{:S(2)}, u32[]{:S(2)}) collective-permute-start(bf16[17,128,128]{2,1,0:T(8,128)(2,1)S(1)} %note.1.p_ref.own_ref.own), channel_id=1, source_target_pairs={{2,3},{3,2},{1,0},{0,1},{4,5},{5,4},{7,6},{6,7},{10,11},{11,10},{9... | collective-permute-start | bytes 1671176 | tf_op jit(solution)/shard_map/ppermute | solution.py:43
  6.8 0.7 %copy-start.4 = (s32[2,2]{1,0:T(2,128)S(1)}, s32[2,2]{1,0:T(2,128)}, u32[]{:S(2)}) copy-start(s32[2,2]{1,0:T(2,128)} %send_ref.1) | copy-start | bytes 52
  8.3 3.3 %collective-permute-start = (bf16[3,128,128]{2,1,0:T(8,128)(2,1)S(1)}, bf16[3,128,128]{2,1,0:T(8,128)(2,1)S(1)}, u32[]{:S(2)}, u32[]{:S(2)}) collective-permute-start(bf16[3,128,128]{2,1,0:T(8,128)(2,1)S(1)} %get-tuple-element.13), channel_id=1, source_target_pairs={{0,4},{4,0},{8,12},{12,8},{16,20},{20,16},{24,28},{28,24},{32,36},... | collective-permute-start | bytes 294920 | tf_op jit(solution)/shard_map/ppermute | solution.py:48
  10.7 4.3 %collective-permute-start.1 = (bf16[3,128,128]{2,1,0:T(8,128)(2,1)S(1)}, bf16[3,128,128]{2,1,0:T(8,128)(2,1)S(1)}, u32[]{:S(2)}, u32[]{:S(2)}) collective-permute-start(bf16[3,128,128]{2,1,0:T(8,128)(2,1)S(1)} %get-tuple-element.14), channel_id=1, source_target_pairs={{0,252},{4,8},{8,4},{12,16},{16,12},{20,24},{24,20},{28,32},{32,28... | collective-permute-start | bytes 294920 | tf_op jit(solution)/shard_map/ppermute | solution.py:48
  15.1 0.7 %copy-start.1 = (s32[16,27]{1,0:T(8,128)S(1)}, s32[16,27]{1,0:T(8,128)}, u32[]{:S(2)}) copy-start(s32[16,27]{1,0:T(8,128)} %cols_ref.1) | copy-start | bytes 5188
  15.8 0.7 %copy-start.3 = (s32[16,1]{0,1:T(1,128)S(1)}, s32[16,1]{0,1:T(1,128)}, u32[]{:S(2)}) copy-start(s32[16,1]{0,1:T(1,128)} %param.8) | copy-start | bytes 196
  33.3 12.4 %collective-permute-start.6 = (bf16[2,384,128]{2,1,0:T(8,128)(2,1)S(1)}, bf16[2,384,128]{2,1,0:T(8,128)(2,1)S(1)}, u32[]{:S(2)}, u32[]{:S(2)}) collective-permute-start(bf16[2,384,128]{2,1,0:T(8,128)(2,1)S(1)} %get-tuple-element.19), channel_id=1, source_target_pairs={{0,252},{4,8},{8,4},{12,16},{16,12},{20,24},{24,20},{28,32},{32,28... | collective-permute-start | bytes 589832 | tf_op jit(solution)/shard_map/ppermute | solution.py:48
  35.8 10.0 %collective-permute-start.5 = (bf16[2,384,128]{2,1,0:T(8,128)(2,1)S(1)}, bf16[2,384,128]{2,1,0:T(8,128)(2,1)S(1)}, u32[]{:S(2)}, u32[]{:S(2)}) collective-permute-start(bf16[2,384,128]{2,1,0:T(8,128)(2,1)S(1)} %get-tuple-element.17.after), channel_id=1, source_target_pairs={{0,4},{4,0},{8,12},{12,8},{16,20},{20,16},{24,28},{28,24},{32,36},... | collective-permute-start | bytes 589832 | tf_op jit(solution)/shard_map/ppermute | solution.py:48

commit v3 on v1

--- a/solution.py
+++ b/solution.py
@@ -123,65 +123,57 @@
     return jnp.concatenate([ref[i] for i in range(BR)], axis=1)
 
 
-def partial_kernel(sums_ref, own, swapped, across, crossed, near_ref, far_ref, tiles, masked, sems):
-    s, is_n, number, first = place()
-
-    @pl.when(is_n)
-    def _():
-        for n, src in enumerate((own, swapped)):
-            pltpu.make_async_copy(src, tiles.at[n], sems.at[n]).start()
-
-    @pl.when(jnp.logical_not(is_n))
-    def _():
-        for n, src in enumerate((across, crossed)):
-            pltpu.make_async_copy(src, tiles.at[n], sems.at[n]).start()
-
-    sums = wide(sums_ref)
+def partial_kernel(sums_ref, own, swapped, across, crossed, near_ref, far_ref, masked):
+    s, is_n, number, first = place()
     odd = lax.rem(s, 2) == 1
-    first_row = jnp.where(is_n, number, 1 - number)
-    for n in range(2):
-        pltpu.make_async_copy(own, tiles.at[n], sems.at[n]).wait()
-        row = first_row if n == 0 else 1 - first_row
+
+    def add(tiles, row, n):
         wanted = lax.rem(2 * s - 2 + row + T, T).astype(F32)
         for i in range(BR):
-            lower = tiles[n, BR, 8 * i:8 * i + 8, :].astype(F32)[:1] == wanted
-            tile = tiles[n, i].astype(F32)
-            masked[n, i * T:(i + 1) * T, :T] = jnp.where(lower, tile, 0.0).astype(BF16)
-            masked[n, i * T:(i + 1) * T, T:] = jnp.where(lower, 0.0, tile).astype(BF16)
-        terms = jnp.dot(sums, masked[n], preferred_element_type=F32)
+            lower = jnp.where(tiles[BR, 8 * i:8 * i + 8, :].astype(F32)[:1] == wanted, 1.0, 0.0)
+            masked[n, i * T:(i + 1) * T, :T] = tiles[i] * lower.astype(BF16)
+            masked[n, i * T:(i + 1) * T, T:] = tiles[i] * (1.0 - lower).astype(BF16)
+        terms = jnp.dot(wide(sums_ref), masked[n], preferred_element_type=F32)
         near_ref[row] = jnp.where(odd, terms[:, :T], terms[:, T:]).astype(BF16)
         far_ref[row] = jnp.where(odd, terms[:, T:], terms[:, :T]).astype(BF16)
 
-
-def local_kernel(sums_ref, rest_ref, own, swapped, across, crossed, after, out_ref, total_ref, tiles, zeros, sems):
+    @pl.when(is_n)
+    def _():
+        add(own, number, 0)
+        add(swapped, 1 - number, 1)
+
+    @pl.when(jnp.logical_not(is_n))
+    def _():
+        add(across, 1 - number, 0)
+        add(crossed, number, 1)
+
+
+def local_kernel(sums_ref, rest_ref, own, swapped, across, crossed, after, out_ref, total_ref, zeros, sems):
     del after
     s, is_n, number, first = place()
-
-    @pl.when(is_n)
-    def _():
-        for n, src in enumerate((across, crossed)):
-            pltpu.make_async_copy(src, tiles.at[n], sems.at[n]).start()
-
-    @pl.when(jnp.logical_not(is_n))
-    def _():
-        for n, src in enumerate((own, swapped)):
-            pltpu.make_async_copy(src, tiles.at[n], sems.at[n]).start()
-
     zeros[...] = jnp.zeros_like(zeros)
-    copies = [pltpu.make_async_copy(zeros, out_ref.at[r, pl.ds(q, 8)], sems.at[2 + r * 4 + q // 8])
+    copies = [pltpu.make_async_copy(zeros, out_ref.at[r, pl.ds(q, 8)], sems.at[r * 4 + q // 8])
               for r in range(2) for q in range(0, NCC, 8)]
     for copy in copies:
         copy.start()
     total_ref[...] = jnp.zeros_like(total_ref)
-    sums = wide(sums_ref)
     at = pl.ds(pl.multiple_of(is_n.astype(jnp.int32) * T, T), G * T)
-    first_row = jnp.where(is_n, 1 - number, number)
-    for n in range(2):
-        pltpu.make_async_copy(own, tiles.at[n], sems.at[n]).wait()
-        right = tiles[n, :BR].reshape(BR * T, T)
-        row = first_row if n == 0 else 1 - first_row
-        total_ref[row, at, :] = (jnp.dot(sums, right, preferred_element_type=F32)
-                                 + jnp.dot(wide(rest_ref), right, preferred_element_type=F32))
+
+    def add(one, other, row):
+        right = jnp.concatenate([x[:BR].reshape(BR * T, T) for x in (one, other)], axis=1)
+        terms = jnp.dot(wide(sums_ref), right, preferred_element_type=F32)
+        terms += jnp.dot(wide(rest_ref), right, preferred_element_type=F32)
+        total_ref[row, at, :] = terms[:, :T]
+        total_ref[1 - row, at, :] = terms[:, T:]
+
+    @pl.when(is_n)
+    def _():
+        add(across, crossed, 1 - number)
+
+    @pl.when(jnp.logical_not(is_n))
+    def _():
+        add(own, swapped, number)
+
     for copy in copies:
         copy.wait()
 
@@ -246,18 +238,16 @@
     )(a_cols, ids, a_tiles, noted, near, far)
     travels = jax.ShapeDtypeStruct((2, G * T, T), BF16)
     near, far = pl.pallas_call(
-        partial_kernel, out_shape=(travels, travels), in_specs=[VMEM] + [HBM] * 4, out_specs=(VMEM, VMEM),
-        scratch_shapes=[pltpu.VMEM((2, BR + 1, T, T), BF16), pltpu.VMEM((2, BR * T, 2 * T), BF16),
-                        pltpu.SemaphoreType.DMA((2,))],
+        partial_kernel, out_shape=(travels, travels), in_specs=[VMEM] * 5, out_specs=(VMEM, VMEM),
+        scratch_shapes=[pltpu.VMEM((2, BR * T, 2 * T), BF16)],
         compiler_params=params(24), name="partials",
     )(sums, noted, swapped, across, crossed)
     near_sum, far_sum = swap_rows(near, 0, rows, cols), swap_rows(far, 1, rows, cols)
     out = jax.ShapeDtypeStruct((2, NCC, T, T), F32)
     zeroed, total = pl.pallas_call(
         local_kernel, out_shape=(out, jax.ShapeDtypeStruct((2, 4 * T, T), F32)),
-        in_specs=[VMEM] * 2 + [HBM] * 5, out_specs=(HBM, VMEM),
-        scratch_shapes=[pltpu.VMEM((2, BR + 1, T, T), BF16), pltpu.VMEM((8, T, T), F32),
-                        pltpu.SemaphoreType.DMA((10,))],
+        in_specs=[VMEM] * 6 + [HBM], out_specs=(HBM, VMEM),
+        scratch_shapes=[pltpu.VMEM((8, T, T), F32), pltpu.SemaphoreType.DMA((8,))],
         compiler_params=params(24), name="local",
     )(sums, rest, noted, swapped, across, crossed, near)
     return pl.pallas_call(

time: 48.6 us -> 45.8 us (0.942)
  Pallas kernels: 22.8 us -> 19.8 us
    pallas_call x1, Pallas kernels: 3.95 us -> 2.1 us  [shards(): pl.pallas_call(local_kernel, out_shape=(out, jax.ShapeDtypeStruct((2, 4 *...]
    pallas_call x1, Pallas kernels: 2.31 us -> 1.1 us  [shards(): pl.pallas_call(partial_kernel, out_shape=(travels, travels), in_specs=[VM...]
  transfers between devices with their start and end apart: 7 -> 7, of which waited for: 3 -> 3; matrix products, arithmetic and copies ran while one was open for 0% -> 0% of each run, Pallas kernels for 39% -> 38%
where the time goes in v3:
time: 45.8 us; the launch traced here: 45.3 us
  Pallas kernels  19.8 us (43%)
  starting transfers between devices  17.6 us (38%)
  waiting for transfers between devices  4.17 us (9%)
  local copies, waits for them, and re-layouts  3.73 us (8%)
    pallas_call x1, Pallas kernels, shards(): pl.pallas_call(product_kernel, out_shape=(turned, turned), in_specs=[SMEM...  14.2 us
    ppermute x4, starting transfers between devices, swap_rows(): return lax.ppermute(block, 'row', pairs)  13.1 us
    ppermute x3, starting transfers between devices, send(): return lax.ppermute(block, ('row', 'col'), pairs)  4.52 us
    ppermute x4, waiting for transfers between devices, swap_rows(): return lax.ppermute(block, 'row', pairs)  3.78 us
    unnamed x10, local copies, waits for them, and re-layouts  3.73 us
    pallas_call x1, Pallas kernels, shards(): pl.pallas_call(local_kernel, out_shape=(out, jax.ShapeDtypeStruct((2, 4 *...  2.1 us
    pallas_call x1, Pallas kernels, shards(): pl.pallas_call(partial_kernel, out_shape=(travels, travels), in_specs=[VM...  1.1 us
    pallas_call x1, Pallas kernels, shards(): pl.pallas_call(final_kernel, out_shape=out, in_specs=[VMEM] * 3 + [HBM],...  0.97 us
  transfers between devices with their start and end apart: 7, of which 3 were waited for; matrix products, arithmetic and copies ran while one was open for 0% of the time, Pallas kernels for 38%

profile of v3, /device:TPU:1, one launch (start us, length us, event | category | flops | bytes accessed | tf_op | source)
XLA Modules:
  0.0 45.3 jit_solution(10855032296949435173)
XLA Ops:
  0.0 0.0 copy-start
  0.0 1.0 %copy-done = bf16[16,1,128,128]{3,2,1,0:T(8,128)(2,1)S(1)} copy-done((bf16[16,1,128,128]{3,2,1,0:T(8,128)(2,1)S(1)}, bf16[16,1,128,128]{3,2,1,0:T(8,128)(2,1)}, u32[]{:S(2)}) %copy-start) | copy-done | bytes 524312
  1.0 0.0 copy-start.2
  1.0 0.7 %copy-done.2 = s32[16,1]{0,1:T(1,128)S(1)} copy-done((s32[16,1]{0,1:T(1,128)S(1)}, s32[16,1]{0,1:T(1,128)}, u32[]{:S(2)}) %copy-start.2) | copy-done | bytes 88
  1.7 0.6 %note.1.p_ref.own_ref.own = bf16[17,128,128]{2,1,0:T(8,128)(2,1)S(1)} custom-call(s32[16]{0:T(128)S(1)} %bitcast.3, bf16[16,128,128]{2,1,0:T(8,128)(2,1)S(1)} %bitcast.2), custom_call_target="tpu_custom_call" | custom-call | tf_op jit(solution)/shard_map/note/pallas_call | solution.py:217
  2.3 3.7 %collective-permute-start.4 = (bf16[17,128,128]{2,1,0:T(8,128)(2,1)S(1)}, bf16[17,128,128]{2,1,0:T(8,128)(2,1)S(1)}, u32[]{:S(2)}, u32[]{:S(2)}) collective-permute-start(bf16[17,128,128]{2,1,0:T(8,128)(2,1)S(1)} %note.1.p_ref.own_ref.own), channel_id=1, source_target_pairs={{2,0},{3,1},{1,3},{0,2},{4,6},{5,7},{7,5},{6,4},{10,8},{11,9},{9,1... | collective-permute-start | bytes 1671176 | tf_op jit(solution)/shard_map/ppermute | solution.py:43
  6.0 0.9 %collective-permute-start.3 = (bf16[17,128,128]{2,1,0:T(8,128)(2,1)S(1)}, bf16[17,128,128]{2,1,0:T(8,128)(2,1)S(1)}, u32[]{:S(2)}, u32[]{:S(2)}) collective-permute-start(bf16[17,128,128]{2,1,0:T(8,128)(2,1)S(1)} %note.1.p_ref.own_ref.own), channel_id=1, source_target_pairs={{2,1},{3,0},{1,2},{0,3},{4,7},{5,6},{7,4},{6,5},{10,9},{11,8},{9,1... | collective-permute-start | bytes 1671176 | tf_op jit(solution)/shard_map/ppermute | solution.py:43
  6.8 0.0 collective-permute-start.2
  6.8 0.0 copy-start.4
  6.8 0.7 %copy-done.4 = s32[2,2]{1,0:T(2,128)S(1)} copy-done((s32[2,2]{1,0:T(2,128)S(1)}, s32[2,2]{1,0:T(2,128)}, u32[]{:S(2)}) %copy-start.4) | copy-done | bytes 40
  7.5 0.8 %pick.1 = (bf16[3,128,128]{2,1,0:T(8,128)(2,1)S(1)}, bf16[3,128,128]{2,1,0:T(8,128)(2,1)S(1)}) custom-call(s32[2,2]{1,0:T(2,128)S(1)} %copy-done.4, bf16[17,128,128]{2,1,0:T(8,128)(2,1)S(1)} %note.1.p_ref.own_ref.own), custom_call_target="tpu_custom_call" | custom-call | tf_op jit(solution)/shard_map/pick/pallas_call | solution.py:225
  8.3 2.4 %collective-permute-start = (bf16[3,128,128]{2,1,0:T(8,128)(2,1)S(1)}, bf16[3,128,128]{2,1,0:T(8,128)(2,1)S(1)}, u32[]{:S(2)}, u32[]{:S(2)}) collective-permute-start(bf16[3,128,128]{2,1,0:T(8,128)(2,1)S(1)} %get-tuple-element.13), channel_id=1, source_target_pairs={{0,4},{4,0},{8,12},{12,8},{16,20},{20,16},{24,28},{28,24},{32,36},... | collective-permute-start | bytes 294920 | tf_op jit(solution)/shard_map/ppermute | solution.py:48
  10.7 0.6 %collective-permute-start.1 = (bf16[3,128,128]{2,1,0:T(8,128)(2,1)S(1)}, bf16[3,128,128]{2,1,0:T(8,128)(2,1)S(1)}, u32[]{:S(2)}, u32[]{:S(2)}) collective-permute-start(bf16[3,128,128]{2,1,0:T(8,128)(2,1)S(1)} %get-tuple-element.14), channel_id=1, source_target_pairs={{0,252},{4,8},{8,4},{12,16},{16,12},{20,24},{24,20},{28,32},{32,28... | collective-permute-start | bytes 294920 | tf_op jit(solution)/shard_map/ppermute | solution.py:48
  11.3 0.4 collective-permute-done.near_ref
  11.7 3.4 %collective-permute-done.1.far_ref = bf16[3,128,128]{2,1,0:T(8,128)(2,1)S(1)} collective-permute-done((bf16[3,128,128]{2,1,0:T(8,128)(2,1)S(1)}, bf16[3,128,128]{2,1,0:T(8,128)(2,1)S(1)}, u32[]{:S(2)}, u32[]{:S(2)}) %collective-permute-start.1) | collective-permute-done | bytes 98336 | tf_op jit(solution)/shard_map/ppermute | solution.py:48
  15.1 0.0 copy-start.1
  15.1 0.7 %copy-done.1 = s32[16,27]{1,0:T(8,128)S(1)} copy-done((s32[16,27]{1,0:T(8,128)S(1)}, s32[16,27]{1,0:T(8,128)}, u32[]{:S(2)}) %copy-start.1) | copy-done | bytes 1752
  15.8 0.0 copy-start.3
  15.8 0.7 %copy-done.3 = s32[16,1]{0,1:T(1,128)S(1)} copy-done((s32[16,1]{0,1:T(1,128)S(1)}, s32[16,1]{0,1:T(1,128)}, u32[]{:S(2)}) %copy-start.3) | copy-done | bytes 88
  16.4 14.2 %products.1 = (bf16[16,384,128]{2,1,0:T(8,128)(2,1)S(1)}, bf16[16,384,128]{2,1,0:T(8,128)(2,1)S(1)}) custom-call(s32[16,27]{1,0:T(8,128)S(1)} %copy-done.1, s32[16]{0:T(128)S(1)} %bitcast.4, bf16[16,27,128,128]{3,2,1,0:T(8,128)(2,1)} %a_ref.1, bf16[17,128,128]{2,1,0:T(8,128)(2,1)S(1)} %note.1.p_ref.own_ref.own, ...), custom_call_target="tpu_custom_call" | custom-call | tf_op jit(solution)/shard_map/products/pallas_call | solution.py:231
  30.6 0.0 collective-permute-done.4.crossed
  30.6 0.4 collective-permute-done.3.across
  31.0 0.0 collective-permute-done.2.swapped
  31.0 1.1 %partials.1 = (bf16[2,384,128]{2,1,0:T(8,128)(2,1)S(1)}, bf16[2,384,128]{2,1,0:T(8,128)(2,1)S(1)}) custom-call(bf16[16,384,128]{2,1,0:T(8,128)(2,1)S(1)} %get-tuple-element.15.sums_ref, bf16[17,128,128]{2,1,0:T(8,128)(2,1)S(1)} %note.1.p_ref.own_ref.own, bf16[17,128,128]{2,1,0:T(8,128)(2,1)S(1)} %collective-permute-done.2.swapped, ...), custom_call_target="tpu_custom_call" | custom-call | tf_op jit(solution)/shard_map/partials/pallas_call | solution.py:240
  32.1 2.4 %collective-permute-start.6 = (bf16[2,384,128]{2,1,0:T(8,128)(2,1)S(1)}, bf16[2,384,128]{2,1,0:T(8,128)(2,1)S(1)}, u32[]{:S(2)}, u32[]{:S(2)}) collective-permute-start(bf16[2,384,128]{2,1,0:T(8,128)(2,1)S(1)} %get-tuple-element.19), channel_id=1, source_target_pairs={{0,252},{4,8},{8,4},{12,16},{16,12},{20,24},{24,20},{28,32},{32,28... | collective-permute-start | bytes 589832 | tf_op jit(solution)/shard_map/ppermute | solution.py:48
  34.5 7.7 %collective-permute-start.5 = (bf16[2,384,128]{2,1,0:T(8,128)(2,1)S(1)}, bf16[2,384,128]{2,1,0:T(8,128)(2,1)S(1)}, u32[]{:S(2)}, u32[]{:S(2)}) collective-permute-start(bf16[2,384,128]{2,1,0:T(8,128)(2,1)S(1)} %get-tuple-element.17.after), channel_id=1, source_target_pairs={{0,4},{4,0},{8,12},{12,8},{16,20},{20,16},{24,28},{28,24},{32,36},... | collective-permute-start | bytes 589832 | tf_op jit(solution)/shard_map/ppermute | solution.py:48
  42.2 2.1 %local.1 = (f32[2,32,128,128]{3,2,1,0:T(8,128)}, f32[2,512,128]{2,1,0:T(8,128)S(1)}) custom-call(bf16[16,384,128]{2,1,0:T(8,128)(2,1)S(1)} %get-tuple-element.15.sums_ref, bf16[16,384,128]{2,1,0:T(8,128)(2,1)S(1)} %get-tuple-element.16.rest_ref, bf16[17,128,128]{2,1,0:T(8,128)(2,1)S(1)} %note.1.p_ref.own_ref.own, ...), custom_call_target="tpu_custom_call" | custom-call | tf_op jit(solution)/shard_map/local/pallas_call | solution.py:247
  44.3 0.0 collective-permute-done.6.far_ref
  44.3 0.0 collective-permute-done.5.near_ref
  44.4 1.0 %final.1 = f32[2,32,128,128]{3,2,1,0:T(8,128)} custom-call(f32[2,512,128]{2,1,0:T(8,128)S(1)} %get-tuple-element.18.total_ref, bf16[2,384,128]{2,1,0:T(8,128)(2,1)S(1)} %collective-permute-done.5.near_ref, bf16[2,384,128]{2,1,0:T(8,128)(2,1)S(1)} %collective-permute-done.6.far_ref, ...), custom_call_target="tpu_custom_call", output_to_operand_aliasing={{}: (3, {})} | custom-call | tf_op jit(solution)/shard_map/final/pallas_call | solution.py:253
Async XLA Ops:
  0.0 1.0 %copy-start = (bf16[16,1,128,128]{3,2,1,0:T(8,128)(2,1)S(1)}, bf16[16,1,128,128]{3,2,1,0:T(8,128)(2,1)}, u32[]{:S(2)}) copy-start(bf16[16,1,128,128]{3,2,1,0:T(8,128)(2,1)} %param.7) | copy-start | bytes 1572868
  1.0 0.7 %copy-start.2 = (s32[16,1]{0,1:T(1,128)S(1)}, s32[16,1]{0,1:T(1,128)}, u32[]{:S(2)}) copy-start(s32[16,1]{0,1:T(1,128)} %param.8) | copy-start | bytes 196
  2.3 28.3 %collective-permute-start.4 = (bf16[17,128,128]{2,1,0:T(8,128)(2,1)S(1)}, bf16[17,128,128]{2,1,0:T(8,128)(2,1)S(1)}, u32[]{:S(2)}, u32[]{:S(2)}) collective-permute-start(bf16[17,128,128]{2,1,0:T(8,128)(2,1)S(1)} %note.1.p_ref.own_ref.own), channel_id=1, source_target_pairs={{2,0},{3,1},{1,3},{0,2},{4,6},{5,7},{7,5},{6,4},{10,8},{11,9},{9,1... | collective-permute-start | bytes 1671176 | tf_op jit(solution)/shard_map/ppermute | solution.py:43
  6.0 25.0 %collective-permute-start.3 = (bf16[17,128,128]{2,1,0:T(8,128)(2,1)S(1)}, bf16[17,128,128]{2,1,0:T(8,128)(2,1)S(1)}, u32[]{:S(2)}, u32[]{:S(2)}) collective-permute-start(bf16[17,128,128]{2,1,0:T(8,128)(2,1)S(1)} %note.1.p_ref.own_ref.own), channel_id=1, source_target_pairs={{2,1},{3,0},{1,2},{0,3},{4,7},{5,6},{7,4},{6,5},{10,9},{11,8},{9,1... | collective-permute-start | bytes 1671176 | tf_op jit(solution)/shard_map/ppermute | solution.py:43
  6.8 24.2 %collective-permute-start.2 = (bf16[17,128,128]{2,1,0:T(8,128)(2,1)S(1)}, bf16[17,128,128]{2,1,0:T(8,128)(2,1)S(1)}, u32[]{:S(2)}, u32[]{:S(2)}) collective-permute-start(bf16[17,128,128]{2,1,0:T(8,128)(2,1)S(1)} %note.1.p_ref.own_ref.own), channel_id=1, source_target_pairs={{2,3},{3,2},{1,0},{0,1},{4,5},{5,4},{7,6},{6,7},{10,11},{11,10},{9... | collective-permute-start | bytes 1671176 | tf_op jit(solution)/shard_map/ppermute | solution.py:43
  6.8 0.7 %copy-start.4 = (s32[2,2]{1,0:T(2,128)S(1)}, s32[2,2]{1,0:T(2,128)}, u32[]{:S(2)}) copy-start(s32[2,2]{1,0:T(2,128)} %send_ref.1) | copy-start | bytes 52
  8.3 3.3 %collective-permute-start = (bf16[3,128,128]{2,1,0:T(8,128)(2,1)S(1)}, bf16[3,128,128]{2,1,0:T(8,128)(2,1)S(1)}, u32[]{:S(2)}, u32[]{:S(2)}) collective-permute-start(bf16[3,128,128]{2,1,0:T(8,128)(2,1)S(1)} %get-tuple-element.13), channel_id=1, source_target_pairs={{0,4},{4,0},{8,12},{12,8},{16,20},{20,16},{24,28},{28,24},{32,36},... | collective-permute-start | bytes 294920 | tf_op jit(solution)/shard_map/ppermute | solution.py:48
  10.7 4.3 %collective-permute-start.1 = (bf16[3,128,128]{2,1,0:T(8,128)(2,1)S(1)}, bf16[3,128,128]{2,1,0:T(8,128)(2,1)S(1)}, u32[]{:S(2)}, u32[]{:S(2)}) collective-permute-start(bf16[3,128,128]{2,1,0:T(8,128)(2,1)S(1)} %get-tuple-element.14), channel_id=1, source_target_pairs={{0,252},{4,8},{8,4},{12,16},{16,12},{20,24},{24,20},{28,32},{32,28... | collective-permute-start | bytes 294920 | tf_op jit(solution)/shard_map/ppermute | solution.py:48
  15.1 0.7 %copy-start.1 = (s32[16,27]{1,0:T(8,128)S(1)}, s32[16,27]{1,0:T(8,128)}, u32[]{:S(2)}) copy-start(s32[16,27]{1,0:T(8,128)} %cols_ref.1) | copy-start | bytes 5188
  15.8 0.7 %copy-start.3 = (s32[16,1]{0,1:T(1,128)S(1)}, s32[16,1]{0,1:T(1,128)}, u32[]{:S(2)}) copy-start(s32[16,1]{0,1:T(1,128)} %param.8) | copy-start | bytes 196
  32.1 12.2 %collective-permute-start.6 = (bf16[2,384,128]{2,1,0:T(8,128)(2,1)S(1)}, bf16[2,384,128]{2,1,0:T(8,128)(2,1)S(1)}, u32[]{:S(2)}, u32[]{:S(2)}) collective-permute-start(bf16[2,384,128]{2,1,0:T(8,128)(2,1)S(1)} %get-tuple-element.19), channel_id=1, source_target_pairs={{0,252},{4,8},{8,4},{12,16},{16,12},{20,24},{24,20},{28,32},{32,28... | collective-permute-start | bytes 589832 | tf_op jit(solution)/shard_map/ppermute | solution.py:48
  34.5 9.8 %collective-permute-start.5 = (bf16[2,384,128]{2,1,0:T(8,128)(2,1)S(1)}, bf16[2,384,128]{2,1,0:T(8,128)(2,1)S(1)}, u32[]{:S(2)}, u32[]{:S(2)}) collective-permute-start(bf16[2,384,128]{2,1,0:T(8,128)(2,1)S(1)} %get-tuple-element.17.after), channel_id=1, source_target_pairs={{0,4},{4,0},{8,12},{12,8},{16,20},{20,16},{24,28},{28,24},{32,36},... | collective-permute-start | bytes 589832 | tf_op jit(solution)/shard_map/ppermute | solution.py:48
